TPU v7x, 512 devices: a whole 4x4x16 slice. The times are simulated.
512 devices in a mesh: seq: 128 (over z, y, core), hid: 4 (over x).
Axes of the slice: x: 4, y: 4, z: 16, core: 2. Of those that a mesh axis runs over, the one named last changes fastest.
Arguments:
- glu: bfloat16 [16384, 1024], P('seq', 'hid'), may hold values from -6 to 6
- dw_kernel: float32 [31, 1024], P(None, 'hid'), may hold values from -1 to 1
- bn_scale: float32 [1024], P('hid'), may hold values from 0.5 to 2
- bn_shift: float32 [1024], P('hid'), may hold values from -3 to 3
- pw_out: bfloat16 [1024, 1024], P('hid'), may hold values from -0.1875 to 0.1875
- block_input: bfloat16 [16384, 1024], P('seq'), may hold values from -6 to 6
- ln_gain: float32 [1024], replicated, may hold values from 0.5 to 2
- w_up: bfloat16 [128, 1024, 4096], P('seq', None, 'hid'), may hold values from -0.1875 to 0.1875
- w_down: bfloat16 [128, 4096, 1024], P('seq', 'hid'), may hold values from -0.09375 to 0.09375
- routes: int32 [16384, 2], P('seq'), may hold values from 0 to 127, all different within a row; in each aligned block of 128 rows (0 to 127, 128 to 255, ...) at most 6 rows name the same one
- gates: float32 [16384, 2], P('seq'), may hold values from 0.2 to 1
Outputs:
- block_output: bfloat16 [16384, 1024], P('seq', 'hid')
Inputs may be any that keep to these rules, and one draw needn't show every extreme that they name: `routes`: each frame names 2 different experts. Among the frames of one index of seq (aligned blocks of 128 frames) no expert is named more than 6 times, a bound that some block reaches.
All inputs are finite; a program needn't handle non-finite values.
Results may differ from a plain program's by a relative error of at most 0.011.
Values may be sent and summed in bfloat16 or wider, within the bound.
No kernel may reach another device: no remote copies, remote signals or barrier semaphores. Data moves between devices by JAX's collectives and lax.ppermute only.
A program may use at most 64 MiB of HBM per device.

v0:
```python
import jax
import jax.numpy as jnp
from jax import lax
from jax.sharding import PartitionSpec as P


def padded_2(block, sides, width):
    for axis, dim in sides:
        count = lax.axis_size(axis)
        forward = [(i, i + 1) for i in range(count - 1)]
        backward = [(target, source) for source, target in forward]
        low = lax.ppermute(
            lax.slice_in_dim(block, block.shape[dim] - width, None, axis=dim), axis, forward
        )
        high = lax.ppermute(lax.slice_in_dim(block, 0, width, axis=dim), axis, backward)
        block = jnp.concatenate([low, block, high], axis=dim)
    return block


def on_device(
    glu, dw_kernel, bn_scale, bn_shift, pw_out, block_input, ln_gain, w_up, w_down, routes, gates
):
    tok_rows, quarter = glu.shape
    width = block_input.shape[1]
    taps = dw_kernel.shape[0]
    half_span = taps // 2
    padded = padded_2(glu, (("seq", 0),), half_span)
    depth_sum = jnp.zeros((tok_rows, quarter), jnp.float32)
    for offset in range(taps):
        depth_sum = (
            depth_sum + padded[offset : offset + tok_rows].astype(jnp.float32) * dw_kernel[offset]
        )
    activated = jax.nn.silu(depth_sum * bn_scale + bn_shift).astype(jnp.bfloat16)
    conv_total = lax.psum(jnp.dot(activated, pw_out, preferred_element_type=jnp.float32), "hid")
    mixed = block_input.astype(jnp.float32) + conv_total
    average = jnp.mean(mixed, axis=1, keepdims=True)
    centered = mixed - average
    spread = jnp.mean(centered * centered, axis=1, keepdims=True)
    normed = (centered / jnp.sqrt(spread + 1e-05) * ln_gain).astype(jnp.bfloat16)
    owners = lax.axis_size("seq")
    capacity = max(6, 4 * tok_rows // owners)
    choices_per = routes.shape[1]
    flat_routes = routes.reshape(-1)
    onehot = (flat_routes[:, None] == jnp.arange(owners, dtype=jnp.int32)[None, :]).astype(
        jnp.int32
    )
    position = jnp.sum(jnp.cumsum(onehot, axis=0) * onehot, axis=1) - 1
    slot_index = flat_routes * capacity + position
    send_buffer = jnp.zeros((owners * capacity, width), jnp.bfloat16)
    send_buffer = send_buffer.at[slot_index].set(jnp.repeat(normed, choices_per, axis=0))
    up_proj = w_up[0]
    down_proj = w_down[0]
    hid_index = lax.axis_index("hid")
    arrived = lax.all_to_all(send_buffer, "seq", split_axis=0, concat_axis=0, tiled=True)
    preact = jnp.dot(arrived, up_proj, preferred_element_type=jnp.float32)
    hidden = jax.nn.silu(preact).astype(jnp.bfloat16)
    summed = lax.psum_scatter(
        lax.dot_general(
            down_proj, hidden, (((0,), (1,)), ((), ())), preferred_element_type=jnp.float32
        ).astype(jnp.bfloat16),
        "hid",
        scatter_dimension=0,
        tiled=True,
    )
    returned = lax.all_to_all(summed, "seq", split_axis=1, concat_axis=1, tiled=True)
    picked = returned[:, slot_index].astype(jnp.float32).reshape(quarter, tok_rows, choices_per)
    weighted = jnp.sum(picked * gates[None, :, :], axis=2).T
    own_cols = lax.dynamic_slice_in_dim(mixed, hid_index * quarter, quarter, 1)
    return (own_cols + weighted).astype(jnp.bfloat16)


def solution(mesh):
    in_specs = (
        P("seq", "hid"),
        P(None, "hid"),
        P("hid"),
        P("hid"),
        P("hid", None),
        P("seq", None),
        P(),
        P("seq", None, "hid"),
        P("seq", "hid", None),
        P("seq", None),
        P("seq", None),
    )
    out_specs = P("seq", "hid")
    return jax.shard_map(
        on_device, mesh=mesh, in_specs=in_specs, out_specs=out_specs, check_vma=False
    )
```

profile of v0, /device:TPU:32, one launch (start us, length us, event | category | flops | bytes accessed | tf_op | source)
XLA Modules:
  0.0 309.6 jit_solution(221584032900111136)
XLA Ops:
  6.5 0.9 fusion.40
  7.4 3.9 %collective-permute-start.1 = (bf16[15,256]{1,0:T(8,128)(2,1)S(1)}, bf16[15,256]{1,0:T(8,128)(2,1)S(1)}, u32[]{:S(2)}, u32[]{:S(2)}) collective-permute-start(bf16[15,256]{1,0:T(8,128)(2,1)S(1)} %get-tuple-element.7), channel_id=1, source_target_pairs={{4,0},{8,4},{12,8},{16,12},{20,16},{24,20},{28,24},{32,28},{36,32}... | collective-permute-start | bytes 23048 | tf_op jit(solution)/shard_map/ppermute | solution.py:15
  11.3 1.9 collective-permute-start
  13.2 1.0 fusion.41
  14.3 1.0 fusion.42
  15.2 0.8 copy.14
  16.0 0.7 broadcast_multiply_fusion
  17.0 0.2 fusion.16
  17.3 0.8 constant_dynamic-update-slice_fusion.1
  18.4 0.1 mul.466
  18.6 3.8 %fusion.35 = f32[128,1024]{1,0:T(8,128)} fusion(bf16[256,1024]{1,0:T(8,128)(2,1)} %param.15, bf16[128,256]{1,0:T(8,128)(2,1)} %param.11, bf16[15,256]{1,0:T(8,128)(2,1)S(1)} %collective-permute-done, bf16[143,256]{1,0:T(8,128)(2,1)S(1)} %constant_dynamic-update-slice_fusion, f32[256]{0:T(256)} %param.14, f32[256]{0:T(256)} %param.13, f32[256]{0:T(256)S(1)} %bitcast.109, ...), kind=kOutput, calls=%fused_computation.64 | convolution fusion | flops 71827456 | bytes 2139136 | tf_op jit(solution)/shard_map/dot_general | solution.py:34
  22.4 0.2 fusion.17
  22.6 63.5 %all-reduce.2.cloned.1.call-done = f32[128,1024]{1,0:T(8,128)} async-done(((f32[128,1024]{1,0:T(8,128)}), f32[128,1024]{1,0:T(8,128)}) %all-reduce.2.cloned.1.call-update) | async-done | bytes 524304 | tf_op jit(solution)/shard_map/psum | solution.py:34
  86.1 1.2 fusion.39
  87.3 0.2 multiply_reduce_fusion
  87.5 0.1 multiply_convert_fusion.4
  87.7 0.3 broadcast_in_dim.5
  88.0 1.0 reshape.93
  89.0 3.4 %scatter_custom_fusion = bf16[768,1024]{1,0:T(8,128)(2,1)} fusion(s32[256]{0:T(256)S(1)} %bitcast.77, bf16[256,1024]{1,0:T(8,128)(2,1)} %reshape.93, bf16[]{:T(256)} %constant.17.clone.1), kind=kCustom, calls=%fused_computation.9 | custom fusion | bytes 1573376 | tf_op jit(solution)/shard_map/scatter | solution.py:50
  92.4 3.7 %all_to_all.16 = bf16[128,6,1024]{2,1,0:T(8,128)(2,1)} reshape(bf16[768,1024]{1,0:T(8,128)(2,1)} %scatter_custom_fusion) | data formatting | bytes 3145728 | tf_op jit(solution)/shard_map/all_to_all | solution.py:54
  96.1 114.8 %all_to_all.24 = bf16[128,6,1024]{2,1,0:T(8,128)(2,1)} all-to-all(bf16[128,6,1024]{2,1,0:T(8,128)(2,1)} %all_to_all.16), channel_id=1, replica_groups=mesh['seq'=128,'hid'=4] {'seq'}, dimensions={0} | all-to-all | bytes 3145728 | tf_op jit(solution)/shard_map/all_to_all | solution.py:54
  210.9 3.7 %all_to_all.18 = bf16[768,1024]{1,0:T(8,128)(2,1)} reshape(bf16[128,6,1024]{2,1,0:T(8,128)(2,1)} %all_to_all.24) | data formatting | bytes 3145728 | tf_op jit(solution)/shard_map/all_to_all | solution.py:54
  214.6 6.9 %fusion.7 = bf16[1024,768]{0,1:T(8,128)(2,1)} fusion(bf16[1,1024,1024]{2,1,0:T(8,128)(2,1)S(1)} %copy-done, bf16[768,1024]{1,0:T(8,128)(2,1)} %all_to_all.18, bf16[1,1024,1024]{2,1,0:T(8,128)(2,1)} %param.18), kind=kOutput, calls=%fused_computation.8 | convolution fusion | flops 3225944064 | bytes 7340032 | tf_op jit(solution)/shard_map/dot_general | solution.py:58
  221.5 26.5 %reduce-scatter.2.cloned.1.call-done = bf16[256,768]{0,1:T(8,128)(2,1)} async-done(((bf16[1024,768]{0,1:T(8,128)(2,1)}), bf16[256,768]{0,1:T(8,128)(2,1)}) %reduce-scatter.2.cloned.1.call-update) | async-done | bytes 393232 | tf_op jit(solution)/shard_map/reduce_scatter | solution.py:57
  248.0 1.9 all_to_all.19
  250.0 16.4 %all-to-all-start.1 = ((bf16[256,128,6]{0,2,1:T(8,128)(2,1)}), bf16[256,128,6]{0,2,1:T(8,128)(2,1)S(1)}, u32[]{:S(2)}, u32[]{:S(2)}) async-start(bf16[256,128,6]{0,2,1:T(8,128)(2,1)} %all_to_all.19), calls=%async_computation.2 | async-start | bytes 1048576 | tf_op jit(solution)/shard_map/all_to_all | solution.py:65
  266.4 0.7 copy.18
  267.2 32.3 %all-to-all-done.1 = bf16[256,128,6]{0,2,1:T(8,128)(2,1)S(1)} async-done(((bf16[256,128,6]{0,2,1:T(8,128)(2,1)}), bf16[256,128,6]{0,2,1:T(8,128)(2,1)S(1)}, u32[]{:S(2)}, u32[]{:S(2)}) %all-to-all-start.1) | async-done | bytes 393248 | tf_op jit(solution)/shard_map/all_to_all | solution.py:65
  299.6 1.2 gather_fusion
  300.8 0.1 reshape.80
  300.9 1.2 multiply_reduce_fusion.1
  302.2 0.7 fusion.18
  (32 shorter events, 0.9 us)
Async XLA Ops:
  6.5 208.1 %copy-start = (bf16[1,1024,1024]{2,1,0:T(8,128)(2,1)S(1)}, bf16[1,1024,1024]{2,1,0:T(8,128)(2,1)}, u32[]{:S(2)}) copy-start(bf16[1,1024,1024]{2,1,0:T(8,128)(2,1)} %param.19) | copy-start | bytes 6291460
  6.5 79.6 %all-reduce.2.cloned.1.call-start = ((), (), s32[]{:S(2)}) async-start(), calls=%async_computation.3 | async-start | bytes 1048576 | tf_op jit(solution)/shard_map/psum | solution.py:34
  7.4 11.1 %collective-permute-start.1 = (bf16[15,256]{1,0:T(8,128)(2,1)S(1)}, bf16[15,256]{1,0:T(8,128)(2,1)S(1)}, u32[]{:S(2)}, u32[]{:S(2)}) collective-permute-start(bf16[15,256]{1,0:T(8,128)(2,1)S(1)} %get-tuple-element.7), channel_id=1, source_target_pairs={{4,0},{8,4},{12,8},{16,12},{20,16},{24,20},{28,24},{32,28},{36,32}... | collective-permute-start | bytes 23048 | tf_op jit(solution)/shard_map/ppermute | solution.py:15
  11.3 7.2 %collective-permute-start = (bf16[15,256]{1,0:T(8,128)(2,1)S(1)}, bf16[15,256]{1,0:T(8,128)(2,1)S(1)}, u32[]{:S(2)}, u32[]{:S(2)}) collective-permute-start(bf16[15,256]{1,0:T(8,128)(2,1)S(1)} %get-tuple-element.8), channel_id=1, source_target_pairs={{0,4},{4,8},{8,12},{12,16},{16,20},{20,24},{24,28},{28,32},{32,36}... | collective-permute-start | bytes 23048 | tf_op jit(solution)/shard_map/ppermute | solution.py:12
  18.5 67.6 %copy-start.1 = (bf16[128,1024]{1,0:T(8,128)(2,1)S(1)}, bf16[128,1024]{1,0:T(8,128)(2,1)}, u32[]{:S(2)}) copy-start(bf16[128,1024]{1,0:T(8,128)(2,1)} %param.16) | copy-start | bytes 786436
  22.3 65.2 %copy-start.2 = (f32[1024]{0:T(1024)S(1)}, f32[1024]{0:T(1024)}, u32[]{:S(2)}) copy-start(f32[1024]{0:T(1024)} %param.17) | copy-start | bytes 12292
  22.3 225.7 %reduce-scatter.2.cloned.1.call-start = ((), (), s32[]{:S(2)}) async-start(), calls=%async_computation.4 | async-start | bytes 1966080 | tf_op jit(solution)/shard_map/reduce_scatter | solution.py:57
  221.5 44.9 %copy-start.3 = (f32[128,2]{0,1:T(2,128)S(1)}, f32[128,2]{0,1:T(2,128)}, u32[]{:S(2)}) copy-start(f32[128,2]{0,1:T(2,128)} %param.21) | copy-start | bytes 3076
  250.0 49.5 %all-to-all-start.1 = ((bf16[256,128,6]{0,2,1:T(8,128)(2,1)}), bf16[256,128,6]{0,2,1:T(8,128)(2,1)S(1)}, u32[]{:S(2)}, u32[]{:S(2)}) async-start(bf16[256,128,6]{0,2,1:T(8,128)(2,1)} %all_to_all.19), calls=%async_computation.2 | async-start | bytes 1048576 | tf_op jit(solution)/shard_map/all_to_all | solution.py:65
Sparse Core Ops, SparseCore 0:
  22.5 63.6 all-reduce.1
  221.6 26.3 reduce-scatter.1
where the time goes:
time: 311 us; the launch traced here: 310 us
  waiting for transfers between devices  122 us (39%)
  blocking collectives  115 us (37%)
  starting transfers between devices  22.3 us (7%)
  local copies, waits for them, and re-layouts  21.4 us (7%)
  between operations  13.6 us (4%)
  matrix products  10.6 us (3%)
  other arithmetic  4.58 us (1%)
    all_to_all x1, blocking collectives, on_device(): lax.all_to_all(send_buffer, 'seq', split_axis=0, concat_axis=0, tiled=True)  115 us
    psum x1, waiting for transfers between devices, on_device(): lax.psum(jnp.dot(activated, pw_out, preferred_element_type=jnp.float32),...  63.5 us
    all_to_all x1, waiting for transfers between devices, on_device(): lax.all_to_all(summed, 'seq', split_axis=1, concat_axis=1, tiled=True)  32.3 us
    reduce_scatter x1, waiting for transfers between devices, on_device(): lax.psum_scatter(lax.dot_general(down_proj, hidden, (((0,), (1,)), ((), (...  26.5 us
    all_to_all x1, starting transfers between devices, on_device(): lax.all_to_all(summed, 'seq', split_axis=1, concat_axis=1, tiled=True)  16.4 us
    all_to_all x2, local copies, waits for them, and re-layouts, on_device(): lax.all_to_all(send_buffer, 'seq', split_axis=0, concat_axis=0, tiled=True)  7.44 us
    dot_general x1, matrix products, on_device(): lax.dot_general(down_proj, hidden, (((0,), (1,)), ((), ())), preferred_el...  6.88 us
  transfers between devices with their start and end apart: 5, of which 3 were waited for; matrix products, arithmetic and copies ran while one was open for 2% of the time, Pallas kernels for 0%

commit v1 on v0

v1 whole, which is shorter than its diff:
```python
import functools

import jax
import jax.numpy as jnp
from jax import lax
from jax.experimental import pallas as pl
from jax.experimental.pallas import tpu as pltpu
from jax.sharding import Mesh, PartitionSpec as P

Z, Y, C, X = 16, 4, 2, 4
YC = Y * C
ROWS = 128
QUARTER = 256
WIDTH = 1024
TAPS = 31
CAP = 6
EDGE = 16
SLOTS = Z * CAP * YC
BLOCK = Z * CAP
AUX = 8

F32, BF16 = jnp.float32, jnp.bfloat16


def dot(a, b, dims=((1,), (0,))):
    return lax.dot_general(a, b, (dims, ((), ())), preferred_element_type=F32)


def silu(v):
    return v / (1.0 + jnp.exp(-v))


def cost(flops, nbytes):
    return pl.CostEstimate(flops=flops, bytes_accessed=nbytes, transcendentals=0)


def call(body, out_shape, name, flops=10**6, nbytes=10**6, scratch=(), vmem=32 << 20, smem=()):
    def run(*args):
        in_specs = [
            pl.BlockSpec(memory_space=pltpu.SMEM if i in smem else pltpu.VMEM)
            for i in range(len(args))
        ]
        return pl.pallas_call(
            body,
            out_shape=out_shape,
            in_specs=in_specs,
            out_specs=jax.tree.map(lambda _: pl.BlockSpec(memory_space=pltpu.VMEM), out_shape),
            scratch_shapes=list(scratch),
            cost_estimate=cost(flops, nbytes),
            compiler_params=pltpu.CompilerParams(vmem_limit_bytes=vmem),
            name=name,
        )(*args)

    return run


def shape(dims, dtype):
    return jax.ShapeDtypeStruct(dims, dtype)


def lanes_to_rows(row):
    return jnp.transpose(jnp.broadcast_to(row, (ROWS, ROWS)))


def routing_kernel(routes_ref, gates_ref, put_ref, pick_ref, gate_ref):
    routes = routes_ref[...]
    expert = lax.broadcasted_iota(jnp.int32, (ROWS, ROWS), 0)
    frame = lax.broadcasted_iota(jnp.int32, (ROWS, ROWS), 1)
    before = (expert < frame).astype(F32).astype(BF16)
    chosen = [(expert == routes[j : j + 1]).astype(F32) for j in range(2)]
    earlier = dot((chosen[0] + chosen[1]).astype(BF16), before)
    slot_row = lax.broadcasted_iota(jnp.int32, (SLOTS, ROWS), 0)
    slot_lane = lax.broadcasted_iota(jnp.int32, (ROWS, SLOTS), 1)
    put = None
    for j in range(2):
        position = jnp.sum(chosen[j] * earlier, axis=0, keepdims=True).astype(jnp.int32)
        named = routes[j : j + 1]
        slot = (named // YC) * (CAP * YC) + position * YC + named % YC
        here = slot_row == slot
        put = here if put is None else put | here
        slot_col = lanes_to_rows(slot.astype(F32))[:, 0:1].astype(jnp.int32)
        pick_ref[j] = (slot_lane == slot_col).astype(F32).astype(BF16)
        gate_ref[j] = lanes_to_rows(gates_ref[j : j + 1])
    put_ref[...] = put.astype(F32).astype(BF16)


def own_conv_kernel(glu_ref, taps_ref, out_ref, padded):
    padded[0:EDGE] = jnp.zeros((EDGE, QUARTER), F32)
    padded[EDGE + ROWS :] = jnp.zeros((EDGE, QUARTER), F32)
    padded[EDGE : EDGE + ROWS] = glu_ref[...].astype(F32)
    total = None
    for k in range(TAPS):
        term = padded[k + 1 : k + 1 + ROWS] * taps_ref[k : k + 1]
        total = term if total is None else total + term
    out_ref[...] = total


def front_kernel(
    own_ref, low_ref, high_ref, taps_ref, scale_ref, shift_ref, pw_ref, input_ref, out_ref, low, high, depth
):
    low[0:EDGE] = low_ref[...].astype(F32)
    low[EDGE:] = jnp.zeros((2 * EDGE, QUARTER), F32)
    high[0 : 2 * EDGE] = jnp.zeros((2 * EDGE, QUARTER), F32)
    high[2 * EDGE :] = high_ref[...].astype(F32)
    depth[...] = own_ref[...]
    first, last = depth[0:EDGE], depth[ROWS - EDGE :]
    for k in range(TAPS):
        tap = taps_ref[k : k + 1]
        first = first + low[k + 1 : k + 1 + EDGE] * tap
        last = last + high[k + 1 : k + 1 + EDGE] * tap
    depth[0:EDGE] = first
    depth[ROWS - EDGE :] = last
    activated = silu(depth[...] * scale_ref[...] + shift_ref[...]).astype(BF16)
    row_sum = 0.25 * jnp.sum(input_ref[...].astype(F32), axis=1, keepdims=True)
    for x in range(X):
        part = dot(activated, pw_ref[:, x * QUARTER : (x + 1) * QUARTER])
        out_ref[x, 0:ROWS] = part
        row_sum = row_sum + jnp.sum(part, axis=1, keepdims=True)
    sums = jnp.transpose(jnp.broadcast_to(row_sum, (ROWS, ROWS)))
    for x in range(X):
        out_ref[x, ROWS:] = jnp.concatenate([sums[0:AUX], sums[0:AUX]], axis=1)


def dispatch_kernel(x_ref, parts_ref, input_ref, gain_ref, put_ref, mixed_ref, out_ref):
    columns = pl.ds(pl.multiple_of(x_ref[0] * QUARTER, QUARTER), QUARTER)
    mixed = input_ref[:, columns].astype(F32)
    sums = jnp.zeros((AUX, ROWS), F32)
    for x in range(X):
        mixed = mixed + parts_ref[x, 0:ROWS]
        sums = sums + parts_ref[x, ROWS:, 0:ROWS]
    mean = lanes_to_rows(sums[0:1])[:, 0:1] * (1.0 / WIDTH)
    mixed_ref[...] = mixed
    scaled = ((mixed - mean) * gain_ref[:, columns]).astype(BF16)
    out_ref[...] = dot(put_ref[...], scaled).astype(BF16)


def spread_kernel(in_ref, out_ref, wide):
    for half in range(2):
        lanes = slice(half * 128, (half + 1) * 128)
        wide[half] = in_ref[:, lanes].astype(F32)
        for yc in range(YC):
            block = wide[half, pl.ds(yc, BLOCK, stride=YC)].astype(BF16)
            for x in range(X):
                out_ref[yc, x, :, lanes] = block


def expert_kernel(in_ref, gain_ref, up_ref, down_ref, out_ref):
    blocks = in_ref.shape[0]
    rows = jnp.concatenate(
        [in_ref[:, x].reshape(blocks * BLOCK, QUARTER) for x in range(X)], axis=1
    )
    centered = rows.astype(F32) / gain_ref[...]
    spread = jnp.sum(centered * centered, axis=1, keepdims=True) * (1.0 / WIDTH)
    inverse = 1.0 / jnp.sqrt(spread + 1e-05)
    hidden = silu(dot(rows, up_ref[...]) * inverse).astype(BF16)
    result = dot(hidden, down_ref[...]).astype(BF16)
    for x in range(X):
        out_ref[:, x] = result[:, x * QUARTER : (x + 1) * QUARTER].reshape(blocks, BLOCK, QUARTER)


def experts(rows, gain, up, down):
    step = 4
    return pl.pallas_call(
        expert_kernel,
        grid=(YC // step,),
        out_shape=shape((YC, X, BLOCK, QUARTER), BF16),
        in_specs=[
            pl.BlockSpec((step, X, BLOCK, QUARTER), lambda i: (i, 0, 0, 0)),
            pl.BlockSpec((1, WIDTH), lambda i: (0, 0)),
            pl.BlockSpec((WIDTH, WIDTH), lambda i: (0, 0)),
            pl.BlockSpec((WIDTH, WIDTH), lambda i: (0, 0)),
        ],
        out_specs=pl.BlockSpec((step, X, BLOCK, QUARTER), lambda i: (i, 0, 0, 0)),
        cost_estimate=cost(4 * YC * BLOCK * WIDTH * WIDTH, 8 << 20),
        compiler_params=pltpu.CompilerParams(vmem_limit_bytes=40 << 20),
        name="experts",
    )(rows, gain, up, down)


def collect_kernel(in_ref, out_ref, wide):
    for half in range(2):
        lanes = slice(half * 128, (half + 1) * 128)
        for yc in range(YC):
            total = in_ref[yc, 0, :, lanes].astype(F32)
            for x in range(1, X):
                total = total + in_ref[yc, x, :, lanes].astype(F32)
            wide[half, pl.ds(yc, BLOCK, stride=YC)] = total
        out_ref[:, lanes] = wide[half].astype(BF16)


def combine_kernel(in_ref, pick_ref, gate_ref, mixed_ref, out_ref):
    rows = in_ref[...]
    moe = dot(pick_ref[0], rows) * gate_ref[0, :, 0:1]
    moe = moe + dot(pick_ref[1], rows) * gate_ref[1, :, 0:1]
    out_ref[...] = (mixed_ref[...] + moe).astype(BF16)


def exchange(value, axes):
    return lax.all_to_all(value, axes, split_axis=0, concat_axis=0, tiled=True)


def on_device(
    glu, dw_kernel, bn_scale, bn_shift, pw_out, block_input, ln_gain, w_up, w_down, routes, gates
):
    seq = ("z", "y", "c")
    count = Z * Y * C
    low = lax.ppermute(glu[ROWS - EDGE :], seq, [(i, i + 1) for i in range(count - 1)])
    high = lax.ppermute(glu[0:EDGE], seq, [(i + 1, i) for i in range(count - 1)])
    gain = ln_gain.reshape(1, WIDTH)
    hid_index = lax.axis_index("x").astype(jnp.int32).reshape(1)

    put, pick, gate = call(
        routing_kernel,
        (
            shape((SLOTS, ROWS), BF16),
            shape((2, ROWS, SLOTS), BF16),
            shape((2, ROWS, ROWS), F32),
        ),
        "routing",
    )(routes.T, gates.T)
    own = call(
        own_conv_kernel,
        shape((ROWS, QUARTER), F32),
        "own_conv",
        scratch=[pltpu.VMEM((ROWS + 2 * EDGE, QUARTER), F32)],
    )(glu, dw_kernel)
    parts = call(
        front_kernel,
        shape((X, ROWS + AUX, QUARTER), F32),
        "front",
        scratch=[
            pltpu.VMEM((3 * EDGE, QUARTER), F32),
            pltpu.VMEM((3 * EDGE, QUARTER), F32),
            pltpu.VMEM((ROWS, QUARTER), F32),
        ],
    )(
        own,
        low,
        high,
        dw_kernel,
        bn_scale.reshape(1, QUARTER),
        bn_shift.reshape(1, QUARTER),
        pw_out,
        block_input,
    )
    parts = exchange(parts, "x")
    mixed, rows = call(
        dispatch_kernel,
        (shape((ROWS, QUARTER), F32), shape((SLOTS, QUARTER), BF16)),
        "dispatch",
        smem=(0,),
    )(hid_index, parts, block_input, gain, put)
    rows = exchange(rows, "z")
    rows = call(
        spread_kernel,
        shape((YC, X, BLOCK, QUARTER), BF16),
        "spread",
        scratch=[pltpu.VMEM((2, SLOTS, 128), F32)],
    )(rows)
    rows = exchange(rows.reshape(YC * X, BLOCK, QUARTER), ("y", "c", "x"))
    rows = experts(rows.reshape(YC, X, BLOCK, QUARTER), gain, w_up[0], w_down[0])
    rows = exchange(rows.reshape(YC * X, BLOCK, QUARTER), ("y", "c", "x"))
    rows = call(
        collect_kernel,
        shape((SLOTS, QUARTER), BF16),
        "collect",
        scratch=[pltpu.VMEM((2, SLOTS, 128), F32)],
    )(rows.reshape(YC, X, BLOCK, QUARTER))
    rows = exchange(rows, "z")
    return call(combine_kernel, shape((ROWS, QUARTER), BF16), "combine")(rows, pick, gate, mixed)


def solution(mesh):
    chips = Mesh(mesh.devices.reshape(Z, Y, C, X), ("z", "y", "c", "x"))
    seq = ("z", "y", "c")
    in_specs = (
        P(seq, "x"),
        P(None, "x"),
        P("x"),
        P("x"),
        P("x", None),
        P(seq, None),
        P(),
        P(seq, None, "x"),
        P(seq, "x", None),
        P(seq, None),
        P(seq, None),
    )
    return jax.shard_map(
        on_device, mesh=chips, in_specs=in_specs, out_specs=P(seq, "x"), check_vma=False
    )
```

time: 311 us -> 159 us (0.51)
  the two profiles are of different devices: /device:TPU:32 before, /device:TPU:3 now
where the time goes in v1:
time: 159 us; the launch traced here: 158 us
  blocking collectives  123 us (77%)
  starting transfers between devices  13.6 us (9%)
  Pallas kernels  8.19 us (5%)
  waiting for transfers between devices  7.86 us (5%)
  local copies, waits for them, and re-layouts  5.72 us (4%)
    all_to_all x4, blocking collectives, exchange(): return lax.all_to_all(value, axes, split_axis=0, concat_axis=0, tiled=True)  123 us
    all_to_all x1, starting transfers between devices, exchange(): return lax.all_to_all(value, axes, split_axis=0, concat_axis=0, tiled=True)  7.89 us
    all_to_all x1, waiting for transfers between devices, exchange(): return lax.all_to_all(value, axes, split_axis=0, concat_axis=0, tiled=True)  7.86 us
    unnamed x24, local copies, waits for them, and re-layouts  4.96 us
    pallas_call x7, Pallas kernels, run(): pl.pallas_call(body, out_shape=out_shape, in_specs=in_specs, out_specs=ja...  4.32 us
    pallas_call x1, Pallas kernels, experts(): pl.pallas_call(expert_kernel, grid=(YC // step,), out_shape=shape((YC, X,...  3.86 us
  transfers between devices with their start and end apart: 3, of which 1 were waited for; matrix products, arithmetic and copies ran while one was open for 0% of the time, Pallas kernels for 1%

profile of v1, /device:TPU:3, one launch (start us, length us, event | category | flops | bytes accessed | tf_op | source)
XLA Modules:
  0.0 158.0 jit_solution(2869564279445233446)
XLA Ops:
  0.0 0.8 fusion
  0.8 2.6 %collective-permute-start.1 = (bf16[16,256]{1,0:T(8,128)(2,1)S(1)}, bf16[16,256]{1,0:T(8,128)(2,1)S(1)}, u32[]{:S(2)}, u32[]{:S(2)}) collective-permute-start(bf16[16,256]{1,0:T(8,128)(2,1)S(1)} %get-tuple-element.15), channel_id=1, source_target_pairs={{4,0},{8,4},{12,8},{16,12},{20,16},{24,20},{28,24},{32,28},{36,32}... | collective-permute-start | bytes 24584 | tf_op jit(solution)/shard_map/ppermute | solution.py:208
  3.3 3.1 %collective-permute-start = (bf16[16,256]{1,0:T(8,128)(2,1)S(1)}, bf16[16,256]{1,0:T(8,128)(2,1)S(1)}, u32[]{:S(2)}, u32[]{:S(2)}) collective-permute-start(bf16[16,256]{1,0:T(8,128)(2,1)S(1)} %get-tuple-element.16), channel_id=1, source_target_pairs={{0,4},{4,8},{8,12},{12,16},{16,20},{20,24},{24,28},{28,32},{32,36}... | collective-permute-start | bytes 24584 | tf_op jit(solution)/shard_map/ppermute | solution.py:207
  6.5 0.0 copy-start.3
  6.5 0.7 copy-done.3
  7.2 0.8 copy-done.4
  8.1 0.6 own_conv.1.own_ref
  8.6 0.0 collective-permute-done.1.high_ref
  8.6 0.0 collective-permute-done.low_ref
  8.7 0.0 copy-start
  8.7 0.9 copy-done
  9.6 1.0 copy-done.2
  10.7 0.7 copy-done.6
  11.3 0.7 copy-done.7
  12.0 1.4 front.1
  13.4 7.9 %all-to-all-start = ((f32[4,136,256]{2,1,0:T(8,128)}), f32[4,136,256]{2,1,0:T(8,128)S(1)}, u32[]{:S(2)}, u32[]{:S(2)}) async-start(f32[4,136,256]{2,1,0:T(8,128)} %front.1), calls=%async_computation | async-start | bytes 1114112 | tf_op jit(solution)/shard_map/all_to_all | solution.py:199
  21.3 0.0 copy-done.10
  21.3 0.0 copy-done.11
  21.3 0.4 routing.1
  21.7 7.9 %all-to-all-done.parts_ref = f32[4,136,256]{2,1,0:T(8,128)S(1)} async-done(((f32[4,136,256]{2,1,0:T(8,128)}), f32[4,136,256]{2,1,0:T(8,128)S(1)}, u32[]{:S(2)}, u32[]{:S(2)}) %all-to-all-start) | async-done | bytes 557088 | tf_op jit(solution)/shard_map/all_to_all | solution.py:199
  29.5 0.0 copy-done.1
  29.5 0.0 copy-done.5
  29.5 0.4 dispatch.1
  29.9 23.5 %all_to_all.37 = bf16[16,48,256]{2,1,0:T(8,128)(2,1)S(1)} all-to-all(bf16[16,48,256]{2,1,0:T(8,128)(2,1)S(1)} %bitcast.23), channel_id=1, replica_groups=mesh['z'=16,'y'=4,'c'=2,'x'=4] {'z'}, dimensions={0} | all-to-all | bytes 786432 | tf_op jit(solution)/shard_map/all_to_all | solution.py:199
  53.5 0.3 spread.1
  53.8 0.0 copy-start.8
  53.8 42.2 %all_to_all.38 = bf16[32,96,256]{2,1,0:T(8,128)(2,1)S(1)} all-to-all(bf16[32,96,256]{2,1,0:T(8,128)(2,1)S(1)} %bitcast.16), channel_id=1, replica_groups=mesh['z'=16,'y'=4,'c'=2,'x'=4] {'y','c','x'}, dimensions={0} | all-to-all | bytes 3145728 | tf_op jit(solution)/shard_map/all_to_all | solution.py:199
  96.1 3.9 %experts.1 = bf16[8,4,96,256]{3,2,1,0:T(8,128)(2,1)S(1)} custom-call(bf16[8,4,96,256]{3,2,1,0:T(8,128)(2,1)S(1)} %bitcast.18, f32[1,1024]{1,0:T(1,128)S(1)} %bitcast.25, bf16[1024,1024]{1,0:T(8,128)(2,1)S(1)} %bitcast.28, bf16[1024,1024]{1,0:T(8,128)(2,1)S(1)} %bitcast.29), custom_call_target="tpu_custom_call" | custom-call | flops 3221225472 | bytes 8388608 | tf_op jit(solution)/shard_map/experts/pallas_call | solution.py:163
  99.9 26.8 %all_to_all.39 = bf16[32,96,256]{2,1,0:T(8,128)(2,1)S(1)} all-to-all(bf16[32,96,256]{2,1,0:T(8,128)(2,1)S(1)} %bitcast.19), channel_id=1, replica_groups=mesh['z'=16,'y'=4,'c'=2,'x'=4] {'y','c','x'}, dimensions={0} | all-to-all | bytes 3145728 | tf_op jit(solution)/shard_map/all_to_all | solution.py:199
  126.7 0.3 collect.1
  127.1 30.1 %all_to_all.40 = bf16[16,48,256]{2,1,0:T(8,128)(2,1)S(1)} all-to-all(bf16[16,48,256]{2,1,0:T(8,128)(2,1)S(1)} %bitcast.22), channel_id=1, replica_groups=mesh['z'=16,'y'=4,'c'=2,'x'=4] {'z'}, dimensions={0} | all-to-all | bytes 786432 | tf_op jit(solution)/shard_map/all_to_all | solution.py:199
  157.1 0.9 combine.1
  (11 shorter events, 0.0 us)
Async XLA Ops:
  0.0 29.5 %copy-start.1 = (bf16[128,1024]{1,0:T(8,128)(2,1)S(1)}, bf16[128,1024]{1,0:T(8,128)(2,1)}, u32[]{:S(2)}) copy-start(bf16[128,1024]{1,0:T(8,128)(2,1)} %input_ref.3) | copy-start | bytes 786436
  0.8 7.9 %collective-permute-start.1 = (bf16[16,256]{1,0:T(8,128)(2,1)S(1)}, bf16[16,256]{1,0:T(8,128)(2,1)S(1)}, u32[]{:S(2)}, u32[]{:S(2)}) collective-permute-start(bf16[16,256]{1,0:T(8,128)(2,1)S(1)} %get-tuple-element.15), channel_id=1, source_target_pairs={{4,0},{8,4},{12,8},{16,12},{20,16},{24,20},{28,24},{32,28},{36,32}... | collective-permute-start | bytes 24584 | tf_op jit(solution)/shard_map/ppermute | solution.py:208
  3.3 5.3 %collective-permute-start = (bf16[16,256]{1,0:T(8,128)(2,1)S(1)}, bf16[16,256]{1,0:T(8,128)(2,1)S(1)}, u32[]{:S(2)}, u32[]{:S(2)}) collective-permute-start(bf16[16,256]{1,0:T(8,128)(2,1)S(1)} %get-tuple-element.16), channel_id=1, source_target_pairs={{0,4},{4,8},{8,12},{12,16},{16,20},{20,24},{24,28},{28,32},{32,36}... | collective-permute-start | bytes 24584 | tf_op jit(solution)/shard_map/ppermute | solution.py:207
  6.5 0.8 copy-start.3
  7.2 0.8 copy-start.4
  8.1 13.2 %copy-start.10 = (s32[128,2]{0,1:T(2,128)S(1)}, s32[128,2]{0,1:T(2,128)}, u32[]{:S(2)}) copy-start(s32[128,2]{0,1:T(2,128)} %param.20) | copy-start | bytes 3076
  8.1 13.2 %copy-start.11 = (f32[128,2]{0,1:T(2,128)S(1)}, f32[128,2]{0,1:T(2,128)}, u32[]{:S(2)}) copy-start(f32[128,2]{0,1:T(2,128)} %param.21) | copy-start | bytes 3076
  8.1 21.5 %copy-start.5 = (f32[1024]{0:T(1024)S(1)}, f32[1024]{0:T(1024)}, u32[]{:S(2)}) copy-start(f32[1024]{0:T(1024)} %param.17) | copy-start | bytes 12292
  8.7 1.0 copy-start
  9.6 1.0 copy-start.2
  10.7 0.7 copy-start.6
  11.3 0.7 copy-start.7
  13.4 16.2 %all-to-all-start = ((f32[4,136,256]{2,1,0:T(8,128)}), f32[4,136,256]{2,1,0:T(8,128)S(1)}, u32[]{:S(2)}, u32[]{:S(2)}) async-start(f32[4,136,256]{2,1,0:T(8,128)} %front.1), calls=%async_computation | async-start | bytes 1114112 | tf_op jit(solution)/shard_map/all_to_all | solution.py:199
  53.5 42.6 %copy-start.9 = (bf16[1,1024,1024]{2,1,0:T(8,128)(2,1)S(1)}, bf16[1,1024,1024]{2,1,0:T(8,128)(2,1)}, u32[]{:S(2)}) copy-start(bf16[1,1024,1024]{2,1,0:T(8,128)(2,1)} %param.19) | copy-start | bytes 6291460
  53.8 42.3 %copy-start.8 = (bf16[1,1024,1024]{2,1,0:T(8,128)(2,1)S(1)}, bf16[1,1024,1024]{2,1,0:T(8,128)(2,1)}, u32[]{:S(2)}) copy-start(bf16[1,1024,1024]{2,1,0:T(8,128)(2,1)} %param.18) | copy-start | bytes 6291460

commit v2 on v1

--- a/solution.py
+++ b/solution.py
@@ -15,9 +15,11 @@
 TAPS = 31
 CAP = 6
 EDGE = 16
-SLOTS = Z * CAP * YC
-BLOCK = Z * CAP
-AUX = 8
+PARTS = 1
+DEPTH = CAP // PARTS
+SLOTS = Z * DEPTH * YC
+BLOCK = Z * DEPTH
+AUX = 16
 
 F32, BF16 = jnp.float32, jnp.bfloat16
 
@@ -35,16 +37,21 @@
 
 
 def call(body, out_shape, name, flops=10**6, nbytes=10**6, scratch=(), vmem=32 << 20, smem=()):
+    def whole(array):
+        zeros = (0,) * len(array.shape)
+        return pl.BlockSpec(array.shape, lambda i: zeros)
+
     def run(*args):
         in_specs = [
-            pl.BlockSpec(memory_space=pltpu.SMEM if i in smem else pltpu.VMEM)
-            for i in range(len(args))
+            pl.BlockSpec(memory_space=pltpu.SMEM) if i in smem else whole(arg)
+            for i, arg in enumerate(args)
         ]
         return pl.pallas_call(
             body,
+            grid=(1,),
             out_shape=out_shape,
             in_specs=in_specs,
-            out_specs=jax.tree.map(lambda _: pl.BlockSpec(memory_space=pltpu.VMEM), out_shape),
+            out_specs=jax.tree.map(whole, out_shape),
             scratch_shapes=list(scratch),
             cost_estimate=cost(flops, nbytes),
             compiler_params=pltpu.CompilerParams(vmem_limit_bytes=vmem),
@@ -71,17 +78,21 @@
     earlier = dot((chosen[0] + chosen[1]).astype(BF16), before)
     slot_row = lax.broadcasted_iota(jnp.int32, (SLOTS, ROWS), 0)
     slot_lane = lax.broadcasted_iota(jnp.int32, (ROWS, SLOTS), 1)
-    put = None
+    put = [None] * PARTS
     for j in range(2):
         position = jnp.sum(chosen[j] * earlier, axis=0, keepdims=True).astype(jnp.int32)
         named = routes[j : j + 1]
-        slot = (named // YC) * (CAP * YC) + position * YC + named % YC
-        here = slot_row == slot
-        put = here if put is None else put | here
-        slot_col = lanes_to_rows(slot.astype(F32))[:, 0:1].astype(jnp.int32)
-        pick_ref[j] = (slot_lane == slot_col).astype(F32).astype(BF16)
+        for i in range(PARTS):
+            inside = (position >= i * DEPTH) & (position < (i + 1) * DEPTH)
+            slot = ((named // YC) * DEPTH + position - i * DEPTH) * YC + named % YC
+            slot = jnp.where(inside, slot, -1)
+            here = slot_row == slot
+            put[i] = here if put[i] is None else put[i] | here
+            slot_col = lanes_to_rows(slot.astype(F32))[:, 0:1].astype(jnp.int32)
+            pick_ref[i, j] = (slot_lane == slot_col).astype(F32).astype(BF16)
         gate_ref[j] = lanes_to_rows(gates_ref[j : j + 1])
-    put_ref[...] = put.astype(F32).astype(BF16)
+    for i in range(PARTS):
+        put_ref[i] = put[i].astype(F32).astype(BF16)
 
 
 def own_conv_kernel(glu_ref, taps_ref, out_ref, padded):
@@ -98,10 +109,10 @@
 def front_kernel(
     own_ref, low_ref, high_ref, taps_ref, scale_ref, shift_ref, pw_ref, input_ref, out_ref, low, high, depth
 ):
-    low[0:EDGE] = low_ref[...].astype(F32)
+    low[0:EDGE] = low_ref[ROWS - EDGE :].astype(F32)
     low[EDGE:] = jnp.zeros((2 * EDGE, QUARTER), F32)
     high[0 : 2 * EDGE] = jnp.zeros((2 * EDGE, QUARTER), F32)
-    high[2 * EDGE :] = high_ref[...].astype(F32)
+    high[2 * EDGE :] = high_ref[0:EDGE].astype(F32)
     depth[...] = own_ref[...]
     first, last = depth[0:EDGE], depth[ROWS - EDGE :]
     for k in range(TAPS):
@@ -114,24 +125,36 @@
     row_sum = 0.25 * jnp.sum(input_ref[...].astype(F32), axis=1, keepdims=True)
     for x in range(X):
         part = dot(activated, pw_ref[:, x * QUARTER : (x + 1) * QUARTER])
-        out_ref[x, 0:ROWS] = part
+        out_ref[x, 0:ROWS] = part.astype(BF16)
         row_sum = row_sum + jnp.sum(part, axis=1, keepdims=True)
-    sums = jnp.transpose(jnp.broadcast_to(row_sum, (ROWS, ROWS)))
+    sums = jnp.transpose(jnp.broadcast_to(row_sum, (ROWS, ROWS)))[0:8]
+    first = sums.astype(BF16).astype(F32)
+    second = (sums - first).astype(BF16).astype(F32)
+    third = sums - first - second
+    terms = jnp.concatenate(
+        [
+            jnp.concatenate([first, second], axis=1),
+            jnp.concatenate([third, jnp.zeros_like(third)], axis=1),
+        ],
+        axis=0,
+    ).astype(BF16)
     for x in range(X):
-        out_ref[x, ROWS:] = jnp.concatenate([sums[0:AUX], sums[0:AUX]], axis=1)
-
-
-def dispatch_kernel(x_ref, parts_ref, input_ref, gain_ref, put_ref, mixed_ref, out_ref):
+        out_ref[x, ROWS:] = terms
+
+
+def dispatch_kernel(x_ref, parts_ref, input_ref, gain_ref, put_ref, mixed_ref, *out_refs):
     columns = pl.ds(pl.multiple_of(x_ref[0] * QUARTER, QUARTER), QUARTER)
     mixed = input_ref[:, columns].astype(F32)
-    sums = jnp.zeros((AUX, ROWS), F32)
+    sums = jnp.zeros((1, ROWS), F32)
     for x in range(X):
-        mixed = mixed + parts_ref[x, 0:ROWS]
-        sums = sums + parts_ref[x, ROWS:, 0:ROWS]
-    mean = lanes_to_rows(sums[0:1])[:, 0:1] * (1.0 / WIDTH)
+        mixed = mixed + parts_ref[x, 0:ROWS].astype(F32)
+        terms = parts_ref[x, ROWS:].astype(F32)
+        sums = sums + (terms[0:1, 0:ROWS] + terms[0:1, ROWS:] + terms[8:9, 0:ROWS])
+    mean = lanes_to_rows(sums)[:, 0:1] * (1.0 / WIDTH)
     mixed_ref[...] = mixed
     scaled = ((mixed - mean) * gain_ref[:, columns]).astype(BF16)
-    out_ref[...] = dot(put_ref[...], scaled).astype(BF16)
+    for i, out_ref in enumerate(out_refs):
+        out_ref[...] = dot(put_ref[i], scaled).astype(BF16)
 
 
 def spread_kernel(in_ref, out_ref, wide):
@@ -159,7 +182,7 @@
 
 
 def experts(rows, gain, up, down):
-    step = 4
+    step = YC if PARTS > 1 else YC // 2
     return pl.pallas_call(
         expert_kernel,
         grid=(YC // step,),
@@ -188,10 +211,14 @@
         out_ref[:, lanes] = wide[half].astype(BF16)
 
 
-def combine_kernel(in_ref, pick_ref, gate_ref, mixed_ref, out_ref):
-    rows = in_ref[...]
-    moe = dot(pick_ref[0], rows) * gate_ref[0, :, 0:1]
-    moe = moe + dot(pick_ref[1], rows) * gate_ref[1, :, 0:1]
+def combine_kernel(pick_ref, gate_ref, mixed_ref, *refs):
+    out_ref = refs[PARTS]
+    picked = [0.0, 0.0]
+    for i in range(PARTS):
+        rows = refs[i][...]
+        for j in range(2):
+            picked[j] = picked[j] + dot(pick_ref[i, j], rows)
+    moe = picked[0] * gate_ref[0, :, 0:1] + picked[1] * gate_ref[1, :, 0:1]
     out_ref[...] = (mixed_ref[...] + moe).astype(BF16)
 
 
@@ -204,16 +231,16 @@
 ):
     seq = ("z", "y", "c")
     count = Z * Y * C
-    low = lax.ppermute(glu[ROWS - EDGE :], seq, [(i, i + 1) for i in range(count - 1)])
-    high = lax.ppermute(glu[0:EDGE], seq, [(i + 1, i) for i in range(count - 1)])
+    low = lax.ppermute(glu, seq, [(i, i + 1) for i in range(count - 1)])
+    high = lax.ppermute(glu, seq, [(i + 1, i) for i in range(count - 1)])
     gain = ln_gain.reshape(1, WIDTH)
     hid_index = lax.axis_index("x").astype(jnp.int32).reshape(1)
 
     put, pick, gate = call(
         routing_kernel,
         (
-            shape((SLOTS, ROWS), BF16),
-            shape((2, ROWS, SLOTS), BF16),
+            shape((PARTS, SLOTS, ROWS), BF16),
+            shape((PARTS, 2, ROWS, SLOTS), BF16),
             shape((2, ROWS, ROWS), F32),
         ),
         "routing",
@@ -222,12 +249,14 @@
         own_conv_kernel,
         shape((ROWS, QUARTER), F32),
         "own_conv",
+        vmem=60 << 20,
         scratch=[pltpu.VMEM((ROWS + 2 * EDGE, QUARTER), F32)],
     )(glu, dw_kernel)
     parts = call(
         front_kernel,
-        shape((X, ROWS + AUX, QUARTER), F32),
+        shape((X, ROWS + AUX, QUARTER), BF16),
         "front",
+        vmem=60 << 20,
         scratch=[
             pltpu.VMEM((3 * EDGE, QUARTER), F32),
             pltpu.VMEM((3 * EDGE, QUARTER), F32),
@@ -244,30 +273,32 @@
         block_input,
     )
     parts = exchange(parts, "x")
-    mixed, rows = call(
+    mixed, *sent = call(
         dispatch_kernel,
-        (shape((ROWS, QUARTER), F32), shape((SLOTS, QUARTER), BF16)),
+        (shape((ROWS, QUARTER), F32),) + (shape((SLOTS, QUARTER), BF16),) * PARTS,
         "dispatch",
         smem=(0,),
     )(hid_index, parts, block_input, gain, put)
-    rows = exchange(rows, "z")
-    rows = call(
-        spread_kernel,
-        shape((YC, X, BLOCK, QUARTER), BF16),
-        "spread",
-        scratch=[pltpu.VMEM((2, SLOTS, 128), F32)],
-    )(rows)
-    rows = exchange(rows.reshape(YC * X, BLOCK, QUARTER), ("y", "c", "x"))
-    rows = experts(rows.reshape(YC, X, BLOCK, QUARTER), gain, w_up[0], w_down[0])
-    rows = exchange(rows.reshape(YC * X, BLOCK, QUARTER), ("y", "c", "x"))
-    rows = call(
-        collect_kernel,
-        shape((SLOTS, QUARTER), BF16),
-        "collect",
-        scratch=[pltpu.VMEM((2, SLOTS, 128), F32)],
-    )(rows.reshape(YC, X, BLOCK, QUARTER))
-    rows = exchange(rows, "z")
-    return call(combine_kernel, shape((ROWS, QUARTER), BF16), "combine")(rows, pick, gate, mixed)
+    back = []
+    for rows in sent:
+        rows = exchange(rows, "z")
+        rows = call(
+            spread_kernel,
+            shape((YC, X, BLOCK, QUARTER), BF16),
+            "spread",
+            scratch=[pltpu.VMEM((2, SLOTS, 128), F32)],
+        )(rows)
+        rows = exchange(rows.reshape(YC * X, BLOCK, QUARTER), ("y", "c", "x"))
+        rows = experts(rows.reshape(YC, X, BLOCK, QUARTER), gain, w_up[0], w_down[0])
+        rows = exchange(rows.reshape(YC * X, BLOCK, QUARTER), ("y", "c", "x"))
+        rows = call(
+            collect_kernel,
+            shape((SLOTS, QUARTER), BF16),
+            "collect",
+            scratch=[pltpu.VMEM((2, SLOTS, 128), F32)],
+        )(rows.reshape(YC, X, BLOCK, QUARTER))
+        back.append(exchange(rows, "z"))
+    return call(combine_kernel, shape((ROWS, QUARTER), BF16), "combine")(pick, gate, mixed, *back)
 
 
 def solution(mesh):

time: 159 us -> 154 us (0.969)
  local copies, waits for them, and re-layouts: 5.72 us -> 0.66 us
  waiting for transfers between devices: 7.86 us -> 4.76 us
  Pallas kernels: 8.19 us -> 10.9 us
    unnamed x24 -> x16, local copies, waits for them, and re-layouts: 4.96 us -> 0.66 us
    all_to_all x1, waiting for transfers between devices: 7.86 us -> 4.76 us  [exchange(): return lax.all_to_all(value, axes, split_axis=0, concat_axis=0, tiled=True)]
    pallas_call x7, Pallas kernels: 4.32 us -> 7.04 us  [run(): pl.pallas_call(body, grid=(1,), out_shape=out_shape, in_specs=in_specs, o...]
  transfers between devices with their start and end apart: 3 -> 3, of which waited for: 1 -> 1; matrix products, arithmetic and copies ran while one was open for 0% -> 0% of each run, Pallas kernels for 1% -> 2%
where the time goes in v2:
time: 154 us
  blocking collectives  124 us (81%)
  starting transfers between devices  13.7 us (9%)
  Pallas kernels  10.9 us (7%)
  waiting for transfers between devices  4.76 us (3%)
    all_to_all x4, blocking collectives, exchange(): return lax.all_to_all(value, axes, split_axis=0, concat_axis=0, tiled=True)  124 us
    all_to_all x1, starting transfers between devices, exchange(): return lax.all_to_all(value, axes, split_axis=0, concat_axis=0, tiled=True)  7.85 us
    pallas_call x7, Pallas kernels, run(): pl.pallas_call(body, grid=(1,), out_shape=out_shape, in_specs=in_specs, o...  7.04 us
    all_to_all x1, waiting for transfers between devices, exchange(): return lax.all_to_all(value, axes, split_axis=0, concat_axis=0, tiled=True)  4.76 us
    pallas_call x1, Pallas kernels, experts(): pl.pallas_call(expert_kernel, grid=(YC // step,), out_shape=shape((YC, X,...  3.86 us
    ppermute x1, starting transfers between devices, on_device(): low = lax.ppermute(glu, seq, [(i, i + 1) for i in range(count - 1)])  3.1 us
  transfers between devices with their start and end apart: 3, of which 1 were waited for; matrix products, arithmetic and copies ran while one was open for 0% of the time, Pallas kernels for 2%

profile of v2, /device:TPU:3, one launch (start us, length us, event | category | flops | bytes accessed | tf_op | source)
XLA Modules:
  0.0 154.0 jit_solution(2923662148842532942)
XLA Ops:
  0.0 0.0 copy-start
  0.0 0.0 copy-start.5
  0.0 0.0 copy-start.4
  0.0 0.0 copy-start.1
  0.0 2.7 %collective-permute-start.1 = (bf16[128,256]{1,0:T(8,128)(2,1)}, bf16[128,256]{1,0:T(8,128)(2,1)S(1)}, u32[]{:S(2)}, u32[]{:S(2)}) collective-permute-start(bf16[128,256]{1,0:T(8,128)(2,1)} %glu_ref.1), channel_id=1, source_target_pairs={{4,0},{8,4},{12,8},{16,12},{20,16},{24,20},{28,24},{32,28},{36,32}... | collective-permute-start | bytes 196616 | tf_op jit(solution)/shard_map/ppermute | solution.py:235
  2.7 3.1 %collective-permute-start = (bf16[128,256]{1,0:T(8,128)(2,1)}, bf16[128,256]{1,0:T(8,128)(2,1)S(1)}, u32[]{:S(2)}, u32[]{:S(2)}) collective-permute-start(bf16[128,256]{1,0:T(8,128)(2,1)} %glu_ref.1), channel_id=1, source_target_pairs={{0,4},{4,8},{8,12},{12,16},{16,20},{20,24},{24,28},{28,32},{32,36}... | collective-permute-start | bytes 196616 | tf_op jit(solution)/shard_map/ppermute | solution.py:234
  5.9 2.1 %own_conv.1.own_ref = f32[128,256]{1,0:T(8,128)} custom-call(bf16[128,256]{1,0:T(8,128)(2,1)} %glu_ref.1, f32[31,256]{1,0:T(8,128)} %taps_ref.3), custom_call_target="tpu_custom_call" | custom-call | flops 1000000 | bytes 1000000 | tf_op jit(solution)/shard_map/own_conv/pallas_call | solution.py:49
  7.9 0.0 collective-permute-done.1.high_ref
  7.9 0.0 collective-permute-done.low_ref
  7.9 0.0 copy-start.7
  8.0 0.6 copy-done.6
  8.6 0.0 copy-done.7
  8.6 2.6 %front.1 = bf16[4,144,256]{2,1,0:T(8,128)(2,1)} custom-call(f32[128,256]{1,0:T(8,128)} %own_conv.1.own_ref, bf16[128,256]{1,0:T(8,128)(2,1)} %copy-done.7, bf16[128,256]{1,0:T(8,128)(2,1)} %copy-done.6, f32[31,256]{1,0:T(8,128)} %taps_ref.3, f32[1,256]{1,0:T(1,128)} %bitcast.30, f32[1,256]{1,0:T(1,128)} %bitcast.31, bf16[256,1024]{1,0:T(8,128)(2,1)} %pw_ref.1, ...), custom_call_target="tpu_custom_call" | custom-call | flops 1000000 | bytes 1000000 | tf_op jit(solution)/shard_map/front/pallas_call | solution.py:49
  11.2 7.8 %all-to-all-start = ((bf16[4,144,256]{2,1,0:T(8,128)(2,1)}), bf16[4,144,256]{2,1,0:T(8,128)(2,1)S(1)}, u32[]{:S(2)}, u32[]{:S(2)}) async-start(bf16[4,144,256]{2,1,0:T(8,128)(2,1)} %front.1), calls=%async_computation | async-start | bytes 589824 | tf_op jit(solution)/shard_map/all_to_all | solution.py:226
  19.0 0.0 copy-done.5
  19.0 0.0 copy-done.4
  19.0 0.4 routing.1
  19.4 4.8 %all-to-all-done.parts_ref = bf16[4,144,256]{2,1,0:T(8,128)(2,1)S(1)} async-done(((bf16[4,144,256]{2,1,0:T(8,128)(2,1)}), bf16[4,144,256]{2,1,0:T(8,128)(2,1)S(1)}, u32[]{:S(2)}, u32[]{:S(2)}) %all-to-all-start) | async-done | bytes 294944 | tf_op jit(solution)/shard_map/all_to_all | solution.py:226
  24.2 0.0 copy-done
  24.2 0.0 copy-done.1
  24.2 0.4 dispatch.1
  24.6 25.2 %all_to_all.37 = bf16[16,48,256]{2,1,0:T(8,128)(2,1)S(1)} all-to-all(bf16[16,48,256]{2,1,0:T(8,128)(2,1)S(1)} %bitcast.23), channel_id=1, replica_groups=mesh['z'=16,'y'=4,'c'=2,'x'=4] {'z'}, dimensions={0} | all-to-all | bytes 786432 | tf_op jit(solution)/shard_map/all_to_all | solution.py:226
  49.8 0.3 spread.1
  50.2 0.0 copy-start.2
  50.2 41.1 %all_to_all.38 = bf16[32,96,256]{2,1,0:T(8,128)(2,1)S(1)} all-to-all(bf16[32,96,256]{2,1,0:T(8,128)(2,1)S(1)} %bitcast.16), channel_id=1, replica_groups=mesh['z'=16,'y'=4,'c'=2,'x'=4] {'y','c','x'}, dimensions={0} | all-to-all | bytes 3145728 | tf_op jit(solution)/shard_map/all_to_all | solution.py:226
  91.3 0.0 copy-done.3
  91.3 0.0 copy-done.2
  91.3 3.9 %experts.1 = bf16[8,4,96,256]{3,2,1,0:T(8,128)(2,1)S(1)} custom-call(bf16[8,4,96,256]{3,2,1,0:T(8,128)(2,1)S(1)} %bitcast.18, f32[1,1024]{1,0:T(1,128)S(1)} %bitcast.25, bf16[1024,1024]{1,0:T(8,128)(2,1)S(1)} %bitcast.26, bf16[1024,1024]{1,0:T(8,128)(2,1)S(1)} %bitcast.27), custom_call_target="tpu_custom_call" | custom-call | flops 3221225472 | bytes 8388608 | tf_op jit(solution)/shard_map/experts/pallas_call | solution.py:186
  95.1 26.8 %all_to_all.39 = bf16[32,96,256]{2,1,0:T(8,128)(2,1)S(1)} all-to-all(bf16[32,96,256]{2,1,0:T(8,128)(2,1)S(1)} %bitcast.19), channel_id=1, replica_groups=mesh['z'=16,'y'=4,'c'=2,'x'=4] {'y','c','x'}, dimensions={0} | all-to-all | bytes 3145728 | tf_op jit(solution)/shard_map/all_to_all | solution.py:226
  121.9 0.3 collect.1
  122.2 30.8 %all_to_all.40 = bf16[16,48,256]{2,1,0:T(8,128)(2,1)S(1)} all-to-all(bf16[16,48,256]{2,1,0:T(8,128)(2,1)S(1)} %bitcast.22), channel_id=1, replica_groups=mesh['z'=16,'y'=4,'c'=2,'x'=4] {'z'}, dimensions={0} | all-to-all | bytes 786432 | tf_op jit(solution)/shard_map/all_to_all | solution.py:226
  153.1 0.9 combine.1
  (2 shorter events, 0.0 us)
Async XLA Ops:
  0.0 24.2 %copy-start = (bf16[128,1024]{1,0:T(8,128)(2,1)S(1)}, bf16[128,1024]{1,0:T(8,128)(2,1)}, u32[]{:S(2)}) copy-start(bf16[128,1024]{1,0:T(8,128)(2,1)} %input_ref.3) | copy-start | bytes 786436
  0.0 19.0 %copy-start.5 = (f32[128,2]{0,1:T(2,128)S(1)}, f32[128,2]{0,1:T(2,128)}, u32[]{:S(2)}) copy-start(f32[128,2]{0,1:T(2,128)} %param.21) | copy-start | bytes 3076
  0.0 19.0 %copy-start.4 = (s32[128,2]{0,1:T(2,128)S(1)}, s32[128,2]{0,1:T(2,128)}, u32[]{:S(2)}) copy-start(s32[128,2]{0,1:T(2,128)} %param.20) | copy-start | bytes 3076
  0.0 24.2 %copy-start.1 = (f32[1024]{0:T(1024)S(1)}, f32[1024]{0:T(1024)}, u32[]{:S(2)}) copy-start(f32[1024]{0:T(1024)} %param.17) | copy-start | bytes 12292
  0.0 7.9 %collective-permute-start.1 = (bf16[128,256]{1,0:T(8,128)(2,1)}, bf16[128,256]{1,0:T(8,128)(2,1)S(1)}, u32[]{:S(2)}, u32[]{:S(2)}) collective-permute-start(bf16[128,256]{1,0:T(8,128)(2,1)} %glu_ref.1), channel_id=1, source_target_pairs={{4,0},{8,4},{12,8},{16,12},{20,16},{24,20},{28,24},{32,28},{36,32}... | collective-permute-start | bytes 196616 | tf_op jit(solution)/shard_map/ppermute | solution.py:235
  2.7 5.2 %collective-permute-start = (bf16[128,256]{1,0:T(8,128)(2,1)}, bf16[128,256]{1,0:T(8,128)(2,1)S(1)}, u32[]{:S(2)}, u32[]{:S(2)}) collective-permute-start(bf16[128,256]{1,0:T(8,128)(2,1)} %glu_ref.1), channel_id=1, source_target_pairs={{0,4},{4,8},{8,12},{12,16},{16,20},{20,24},{24,28},{28,32},{32,36}... | collective-permute-start | bytes 196616 | tf_op jit(solution)/shard_map/ppermute | solution.py:234
  7.9 0.6 copy-start.6
  7.9 0.6 copy-start.7
  11.2 13.0 %all-to-all-start = ((bf16[4,144,256]{2,1,0:T(8,128)(2,1)}), bf16[4,144,256]{2,1,0:T(8,128)(2,1)S(1)}, u32[]{:S(2)}, u32[]{:S(2)}) async-start(bf16[4,144,256]{2,1,0:T(8,128)(2,1)} %front.1), calls=%async_computation | async-start | bytes 589824 | tf_op jit(solution)/shard_map/all_to_all | solution.py:226
  49.8 41.4 %copy-start.3 = (bf16[1,1024,1024]{2,1,0:T(8,128)(2,1)S(1)}, bf16[1,1024,1024]{2,1,0:T(8,128)(2,1)}, u32[]{:S(2)}) copy-start(bf16[1,1024,1024]{2,1,0:T(8,128)(2,1)} %param.19) | copy-start | bytes 6291460
  50.2 41.1 %copy-start.2 = (bf16[1,1024,1024]{2,1,0:T(8,128)(2,1)S(1)}, bf16[1,1024,1024]{2,1,0:T(8,128)(2,1)}, u32[]{:S(2)}) copy-start(bf16[1,1024,1024]{2,1,0:T(8,128)(2,1)} %param.18) | copy-start | bytes 6291460

commit v3 on v2

--- a/solution.py
+++ b/solution.py
@@ -15,10 +15,10 @@
 TAPS = 31
 CAP = 6
 EDGE = 16
-PARTS = 1
-DEPTH = CAP // PARTS
-SLOTS = Z * DEPTH * YC
-BLOCK = Z * DEPTH
+SLOTS = Z * CAP * YC
+BLOCK = Z * CAP
+SHORT = 32
+PACKED = Z * SHORT
 AUX = 16
 
 F32, BF16 = jnp.float32, jnp.bfloat16
@@ -69,30 +69,64 @@
     return jnp.transpose(jnp.broadcast_to(row, (ROWS, ROWS)))
 
 
-def routing_kernel(routes_ref, gates_ref, put_ref, pick_ref, gate_ref):
-    routes = routes_ref[...]
+def ranks(routes):
     expert = lax.broadcasted_iota(jnp.int32, (ROWS, ROWS), 0)
     frame = lax.broadcasted_iota(jnp.int32, (ROWS, ROWS), 1)
     before = (expert < frame).astype(F32).astype(BF16)
     chosen = [(expert == routes[j : j + 1]).astype(F32) for j in range(2)]
-    earlier = dot((chosen[0] + chosen[1]).astype(BF16), before)
-    slot_row = lax.broadcasted_iota(jnp.int32, (SLOTS, ROWS), 0)
-    slot_lane = lax.broadcasted_iota(jnp.int32, (ROWS, SLOTS), 1)
-    put = [None] * PARTS
+    both = chosen[0] + chosen[1]
+    return expert, frame, chosen, both, dot(both.astype(BF16), before)
+
+
+def place(slots, count):
+    row = lax.broadcasted_iota(jnp.int32, (count, ROWS), 0)
+    lane = lax.broadcasted_iota(jnp.int32, (ROWS, count), 1)
+    put = ((row == slots[0]) | (row == slots[1])).astype(F32).astype(BF16)
+    picks = [
+        (lane == lanes_to_rows(slot.astype(F32))[:, 0:1].astype(jnp.int32)).astype(F32).astype(BF16)
+        for slot in slots
+    ]
+    return put, picks
+
+
+def full_routing_kernel(routes_ref, put_ref, pick_ref):
+    routes = routes_ref[...]
+    _, _, chosen, _, earlier = ranks(routes)
+    slots = []
     for j in range(2):
         position = jnp.sum(chosen[j] * earlier, axis=0, keepdims=True).astype(jnp.int32)
         named = routes[j : j + 1]
-        for i in range(PARTS):
-            inside = (position >= i * DEPTH) & (position < (i + 1) * DEPTH)
-            slot = ((named // YC) * DEPTH + position - i * DEPTH) * YC + named % YC
-            slot = jnp.where(inside, slot, -1)
-            here = slot_row == slot
-            put[i] = here if put[i] is None else put[i] | here
-            slot_col = lanes_to_rows(slot.astype(F32))[:, 0:1].astype(jnp.int32)
-            pick_ref[i, j] = (slot_lane == slot_col).astype(F32).astype(BF16)
+        slots.append(((named // YC) * CAP + position) * YC + named % YC)
+    put, picks = place(slots, SLOTS)
+    put_ref[...] = put
+    for j in range(2):
+        pick_ref[j] = picks[j]
+
+
+def routing_kernel(routes_ref, gates_ref, put_ref, counts_ref, pick_ref, gate_ref):
+    routes = routes_ref[...]
+    expert, frame, chosen, both, earlier = ranks(routes)
+    count = jnp.broadcast_to(jnp.sum(both, axis=1, keepdims=True), (ROWS, ROWS))
+    lower = ((frame // YC == expert // YC) & (frame < expert)).astype(F32).astype(BF16)
+    start = dot(lower, count.astype(BF16))
+    too_many = jnp.max(start + count) > SHORT - 1
+    slots = []
+    for j in range(2):
+        rank = jnp.sum(chosen[j] * (earlier + start), axis=0, keepdims=True).astype(jnp.int32)
+        named = routes[j : j + 1]
+        slots.append(jnp.where(rank < SHORT - 1, (named // YC) * SHORT + rank, -1))
         gate_ref[j] = lanes_to_rows(gates_ref[j : j + 1])
-    for i in range(PARTS):
-        put_ref[i] = put[i].astype(F32).astype(BF16)
+    put, picks = place(slots, PACKED)
+    put_ref[...] = put
+    for j in range(2):
+        pick_ref[j] = picks[j]
+    row = lax.broadcasted_iota(jnp.int32, (PACKED, ROWS), 0)
+    named = lax.broadcasted_iota(jnp.int32, (PACKED, ROWS), 1)
+    last = (row == (named // YC) * SHORT + SHORT - 1).astype(F32).astype(BF16)
+    flag = jnp.where(too_many, 1.0, 0.0)
+    values = jnp.where(frame == expert % YC, count, 0.0)
+    values = values + jnp.where((frame == YC) & (expert % YC == 0), flag, 0.0)
+    counts_ref[...] = dot(last, values.astype(BF16)).astype(BF16)
 
 
 def own_conv_kernel(glu_ref, taps_ref, out_ref, padded):
@@ -142,7 +176,9 @@
         out_ref[x, ROWS:] = terms
 
 
-def dispatch_kernel(x_ref, parts_ref, input_ref, gain_ref, put_ref, mixed_ref, *out_refs):
+def dispatch_kernel(
+    x_ref, parts_ref, input_ref, gain_ref, put_ref, counts_ref, mixed_ref, scaled_ref, out_ref
+):
     columns = pl.ds(pl.multiple_of(x_ref[0] * QUARTER, QUARTER), QUARTER)
     mixed = input_ref[:, columns].astype(F32)
     sums = jnp.zeros((1, ROWS), F32)
@@ -153,11 +189,18 @@
     mean = lanes_to_rows(sums)[:, 0:1] * (1.0 / WIDTH)
     mixed_ref[...] = mixed
     scaled = ((mixed - mean) * gain_ref[:, columns]).astype(BF16)
-    for i, out_ref in enumerate(out_refs):
-        out_ref[...] = dot(put_ref[i], scaled).astype(BF16)
-
-
-def spread_kernel(in_ref, out_ref, wide):
+    scaled_ref[...] = scaled
+    out_ref[...] = dot(put_ref[...], scaled).astype(BF16)
+    for z in range(Z):
+        tail = pl.ds(z * SHORT + SHORT - 16, 16)
+        out_ref[tail, 0:ROWS] = out_ref[tail, 0:ROWS] + counts_ref[tail]
+
+
+def full_dispatch_kernel(scaled_ref, put_ref, out_ref):
+    out_ref[...] = dot(put_ref[...], scaled_ref[...]).astype(BF16)
+
+
+def full_spread_kernel(in_ref, out_ref, wide):
     for half in range(2):
         lanes = slice(half * 128, (half + 1) * 128)
         wide[half] = in_ref[:, lanes].astype(F32)
@@ -165,6 +208,31 @@
             block = wide[half, pl.ds(yc, BLOCK, stride=YC)].astype(BF16)
             for x in range(X):
                 out_ref[yc, x, :, lanes] = block
+
+
+def spread_kernel(in_ref, out_ref, source_ref, wide):
+    rows = in_ref[...]
+    wide[...] = rows[:, 0:ROWS].astype(F32)
+    lane = lax.broadcasted_iota(jnp.int32, (Z, ROWS), 1)
+    counts = wide[pl.ds(SHORT - 1, Z, stride=SHORT)]
+    counts = jnp.where(lane < YC, counts, 0.0).astype(BF16)
+    lower = lax.broadcasted_iota(jnp.int32, (ROWS, ROWS), 0)
+    upper = lax.broadcasted_iota(jnp.int32, (ROWS, ROWS), 1)
+    starts = dot(counts, (lower < upper).astype(F32).astype(BF16)).astype(BF16)
+    row = lax.broadcasted_iota(jnp.int32, (BLOCK, Z), 0)
+    sender = (row // CAP == lax.broadcasted_iota(jnp.int32, (BLOCK, Z), 1)).astype(F32).astype(BF16)
+    row = lax.broadcasted_iota(jnp.int32, (BLOCK, ROWS), 0)
+    position = (row % CAP).astype(F32)
+    source = (row // CAP * SHORT).astype(F32) + dot(sender, starts) + position
+    source = jnp.where(position < dot(sender, counts), source, -1.0)
+    packed = lax.broadcasted_iota(jnp.int32, (BLOCK, PACKED), 1).astype(F32)
+    for yc in range(YC):
+        take = (packed == source[:, yc : yc + 1]).astype(F32).astype(BF16)
+        block = dot(take, rows).astype(BF16)
+        for x in range(X):
+            out_ref[yc, x] = block
+    source = jnp.concatenate([source, jnp.full((ROWS - BLOCK, ROWS), -1.0, F32)], axis=0)
+    source_ref[...] = jnp.transpose(source)[0:YC]
 
 
 def expert_kernel(in_ref, gain_ref, up_ref, down_ref, out_ref):
@@ -182,7 +250,7 @@
 
 
 def experts(rows, gain, up, down):
-    step = YC if PARTS > 1 else YC // 2
+    step = YC // 2
     return pl.pallas_call(
         expert_kernel,
         grid=(YC // step,),
@@ -200,25 +268,34 @@
     )(rows, gain, up, down)
 
 
-def collect_kernel(in_ref, out_ref, wide):
+def summed(in_ref, yc, lanes=slice(None)):
+    total = in_ref[yc, 0, :, lanes].astype(F32)
+    for x in range(1, X):
+        total = total + in_ref[yc, x, :, lanes].astype(F32)
+    return total
+
+
+def full_collect_kernel(in_ref, out_ref, wide):
     for half in range(2):
         lanes = slice(half * 128, (half + 1) * 128)
         for yc in range(YC):
-            total = in_ref[yc, 0, :, lanes].astype(F32)
-            for x in range(1, X):
-                total = total + in_ref[yc, x, :, lanes].astype(F32)
-            wide[half, pl.ds(yc, BLOCK, stride=YC)] = total
+            wide[half, pl.ds(yc, BLOCK, stride=YC)] = summed(in_ref, yc, lanes)
         out_ref[:, lanes] = wide[half].astype(BF16)
 
 
-def combine_kernel(pick_ref, gate_ref, mixed_ref, *refs):
-    out_ref = refs[PARTS]
-    picked = [0.0, 0.0]
-    for i in range(PARTS):
-        rows = refs[i][...]
-        for j in range(2):
-            picked[j] = picked[j] + dot(pick_ref[i, j], rows)
-    moe = picked[0] * gate_ref[0, :, 0:1] + picked[1] * gate_ref[1, :, 0:1]
+def collect_kernel(in_ref, source_ref, out_ref):
+    packed = lax.broadcasted_iota(jnp.int32, (PACKED, BLOCK), 0).astype(F32)
+    result = jnp.zeros((PACKED, QUARTER), F32)
+    for yc in range(YC):
+        give = (packed == source_ref[yc : yc + 1, 0:BLOCK]).astype(F32).astype(BF16)
+        result = result + dot(give, summed(in_ref, yc).astype(BF16))
+    out_ref[...] = result.astype(BF16)
+
+
+def combine_kernel(in_ref, pick_ref, gate_ref, mixed_ref, out_ref):
+    rows = in_ref[...]
+    moe = dot(pick_ref[0], rows) * gate_ref[0, :, 0:1]
+    moe = moe + dot(pick_ref[1], rows) * gate_ref[1, :, 0:1]
     out_ref[...] = (mixed_ref[...] + moe).astype(BF16)
 
 
@@ -236,11 +313,12 @@
     gain = ln_gain.reshape(1, WIDTH)
     hid_index = lax.axis_index("x").astype(jnp.int32).reshape(1)
 
-    put, pick, gate = call(
+    put, counts, pick, gate = call(
         routing_kernel,
         (
-            shape((PARTS, SLOTS, ROWS), BF16),
-            shape((PARTS, 2, ROWS, SLOTS), BF16),
+            shape((PACKED, ROWS), BF16),
+            shape((PACKED, ROWS), BF16),
+            shape((2, ROWS, PACKED), BF16),
             shape((2, ROWS, ROWS), F32),
         ),
         "routing",
@@ -273,32 +351,71 @@
         block_input,
     )
     parts = exchange(parts, "x")
-    mixed, *sent = call(
+    mixed, scaled, rows = call(
         dispatch_kernel,
-        (shape((ROWS, QUARTER), F32),) + (shape((SLOTS, QUARTER), BF16),) * PARTS,
+        (
+            shape((ROWS, QUARTER), F32),
+            shape((ROWS, QUARTER), BF16),
+            shape((PACKED, QUARTER), BF16),
+        ),
         "dispatch",
         smem=(0,),
-    )(hid_index, parts, block_input, gain, put)
-    back = []
-    for rows in sent:
-        rows = exchange(rows, "z")
-        rows = call(
+    )(hid_index, parts, block_input, gain, put, counts)
+    rows = exchange(rows, "z")
+    flags = rows.reshape(Z, SHORT, QUARTER)[:, SHORT - 1, YC]
+    crowded = jnp.max(flags.astype(F32)) > 0.5
+
+    def full_slots():
+        return call(
+            full_routing_kernel,
+            (shape((SLOTS, ROWS), BF16), shape((2, ROWS, SLOTS), BF16)),
+            "full_routing",
+        )(routes.T)
+
+    def full_out(_):
+        sent = call(full_dispatch_kernel, shape((SLOTS, QUARTER), BF16), "full_dispatch")(
+            scaled, full_slots()[0]
+        )
+        blocks = call(
+            full_spread_kernel,
+            shape((YC, X, BLOCK, QUARTER), BF16),
+            "full_spread",
+            scratch=[pltpu.VMEM((2, SLOTS, 128), F32)],
+        )(exchange(sent, "z"))
+        return blocks, jnp.zeros((YC, ROWS), F32)
+
+    def short_out(packed):
+        return call(
             spread_kernel,
-            shape((YC, X, BLOCK, QUARTER), BF16),
+            (shape((YC, X, BLOCK, QUARTER), BF16), shape((YC, ROWS), F32)),
             "spread",
+            scratch=[pltpu.VMEM((PACKED, ROWS), F32)],
+        )(packed)
+
+    rows, source = lax.cond(crowded, full_out, short_out, rows)
+    rows = exchange(rows.reshape(YC * X, BLOCK, QUARTER), ("y", "c", "x"))
+    rows = experts(rows.reshape(YC, X, BLOCK, QUARTER), gain, w_up[0], w_down[0])
+    rows = exchange(rows.reshape(YC * X, BLOCK, QUARTER), ("y", "c", "x"))
+    rows = rows.reshape(YC, X, BLOCK, QUARTER)
+
+    def full_back(blocks):
+        sent = call(
+            full_collect_kernel,
+            shape((SLOTS, QUARTER), BF16),
+            "full_collect",
             scratch=[pltpu.VMEM((2, SLOTS, 128), F32)],
-        )(rows)
-        rows = exchange(rows.reshape(YC * X, BLOCK, QUARTER), ("y", "c", "x"))
-        rows = experts(rows.reshape(YC, X, BLOCK, QUARTER), gain, w_up[0], w_down[0])
-        rows = exchange(rows.reshape(YC * X, BLOCK, QUARTER), ("y", "c", "x"))
-        rows = call(
-            collect_kernel,
-            shape((SLOTS, QUARTER), BF16),
-            "collect",
-            scratch=[pltpu.VMEM((2, SLOTS, 128), F32)],
-        )(rows.reshape(YC, X, BLOCK, QUARTER))
-        back.append(exchange(rows, "z"))
-    return call(combine_kernel, shape((ROWS, QUARTER), BF16), "combine")(pick, gate, mixed, *back)
+        )(blocks)
+        return call(combine_kernel, shape((ROWS, QUARTER), BF16), "full_combine")(
+            exchange(sent, "z"), full_slots()[1], gate, mixed
+        )
+
+    def short_back(blocks):
+        sent = call(collect_kernel, shape((PACKED, QUARTER), BF16), "collect")(blocks, source)
+        return call(combine_kernel, shape((ROWS, QUARTER), BF16), "combine")(
+            exchange(sent, "z"), pick, gate, mixed
+        )
+
+    return lax.cond(crowded, full_back, short_back, rows)
 
 
 def solution(mesh):

time: 154 us -> 147 us (0.955)
  the two profiles are of different devices: /device:TPU:3 before, /device:TPU:32 now
where the time goes in v3:
time: 147 us; the launch traced here: 146 us
  blocking collectives  78.7 us (54%)
  starting transfers between devices  26.7 us (18%)
  waiting for transfers between devices  25.1 us (17%)
  Pallas kernels  13.1 us (9%)
    all_to_all x3, blocking collectives, exchange(): return lax.all_to_all(value, axes, split_axis=0, concat_axis=0, tiled=True)  78.7 us
    all_to_all x2, waiting for transfers between devices, exchange(): return lax.all_to_all(value, axes, split_axis=0, concat_axis=0, tiled=True)  21.2 us
    all_to_all x2, starting transfers between devices, exchange(): return lax.all_to_all(value, axes, split_axis=0, concat_axis=0, tiled=True)  20.7 us
    pallas_call x7, Pallas kernels, run(): pl.pallas_call(body, grid=(1,), out_shape=out_shape, in_specs=in_specs, o...  9.24 us
    ppermute x1, starting transfers between devices, on_device(): high = lax.ppermute(glu, seq, [(i + 1, i) for i in range(count - 1)])  4.04 us
    ppermute x1, waiting for transfers between devices, on_device(): low = lax.ppermute(glu, seq, [(i, i + 1) for i in range(count - 1)])  3.91 us
    pallas_call x1, Pallas kernels, experts(): pl.pallas_call(expert_kernel, grid=(YC // step,), out_shape=shape((YC, X,...  3.84 us
  transfers between devices with their start and end apart: 4, of which 3 were waited for; matrix products, arithmetic and copies ran while one was open for 0% of the time, Pallas kernels for 2%

profile of v3, /device:TPU:32, one launch (start us, length us, event | category | flops | bytes accessed | tf_op | source)
XLA Modules:
  0.0 146.3 jit_solution(5023933726592139348)
XLA Ops:
  0.0 0.0 copy-start.1
  0.0 4.0 %collective-permute-start.1 = (bf16[128,256]{1,0:T(8,128)(2,1)}, bf16[128,256]{1,0:T(8,128)(2,1)S(1)}, u32[]{:S(2)}, u32[]{:S(2)}) collective-permute-start(bf16[128,256]{1,0:T(8,128)(2,1)} %glu_ref.1), channel_id=1, source_target_pairs={{4,0},{8,4},{12,8},{16,12},{20,16},{24,20},{28,24},{32,28},{36,32}... | collective-permute-start | bytes 196616 | tf_op jit(solution)/shard_map/ppermute | solution.py:312
  4.1 1.9 %collective-permute-start = (bf16[128,256]{1,0:T(8,128)(2,1)}, bf16[128,256]{1,0:T(8,128)(2,1)S(1)}, u32[]{:S(2)}, u32[]{:S(2)}) collective-permute-start(bf16[128,256]{1,0:T(8,128)(2,1)} %glu_ref.1), channel_id=1, source_target_pairs={{0,4},{4,8},{8,12},{12,16},{16,20},{20,24},{24,28},{28,32},{32,36}... | collective-permute-start | bytes 196616 | tf_op jit(solution)/shard_map/ppermute | solution.py:311
  6.0 2.1 %own_conv.1.own_ref = f32[128,256]{1,0:T(8,128)} custom-call(bf16[128,256]{1,0:T(8,128)(2,1)} %glu_ref.1, f32[31,256]{1,0:T(8,128)} %taps_ref.3), custom_call_target="tpu_custom_call" | custom-call | flops 1000000 | bytes 1000000 | tf_op jit(solution)/shard_map/own_conv/pallas_call | solution.py:49
  8.1 0.0 collective-permute-done.1.high_ref
  8.1 3.9 %collective-permute-done.low_ref = bf16[128,256]{1,0:T(8,128)(2,1)S(1)} collective-permute-done((bf16[128,256]{1,0:T(8,128)(2,1)}, bf16[128,256]{1,0:T(8,128)(2,1)S(1)}, u32[]{:S(2)}, u32[]{:S(2)}) %collective-permute-start) | collective-permute-done | bytes 65568 | tf_op jit(solution)/shard_map/ppermute | solution.py:311
  12.0 0.0 copy-done.6
  12.0 0.6 copy-done.7
  12.6 2.6 %front.1 = bf16[4,144,256]{2,1,0:T(8,128)(2,1)} custom-call(f32[128,256]{1,0:T(8,128)} %own_conv.1.own_ref, bf16[128,256]{1,0:T(8,128)(2,1)} %copy-done.7, bf16[128,256]{1,0:T(8,128)(2,1)} %copy-done.6, f32[31,256]{1,0:T(8,128)} %taps_ref.3, f32[1,256]{1,0:T(1,128)} %bitcast.38, f32[1,256]{1,0:T(1,128)} %bitcast.39, bf16[256,1024]{1,0:T(8,128)(2,1)} %pw_ref.1, ...), custom_call_target="tpu_custom_call" | custom-call | flops 1000000 | bytes 1000000 | tf_op jit(solution)/shard_map/front/pallas_call | solution.py:49
  15.2 4.3 %all-to-all-start.3 = ((bf16[4,144,256]{2,1,0:T(8,128)(2,1)}), bf16[4,144,256]{2,1,0:T(8,128)(2,1)S(1)}, u32[]{:S(2)}, u32[]{:S(2)}) async-start(bf16[4,144,256]{2,1,0:T(8,128)(2,1)} %front.1), calls=%async_computation.3 | async-start | bytes 589824 | tf_op jit(solution)/shard_map/all_to_all | solution.py:303
  19.5 0.0 copy-done.8
  19.5 0.0 copy-done.4
  19.5 0.6 routing.1
  20.1 6.2 %all-to-all-done.3.parts_ref = bf16[4,144,256]{2,1,0:T(8,128)(2,1)S(1)} async-done(((bf16[4,144,256]{2,1,0:T(8,128)(2,1)}), bf16[4,144,256]{2,1,0:T(8,128)(2,1)S(1)}, u32[]{:S(2)}, u32[]{:S(2)}) %all-to-all-start.3) | async-done | bytes 294944 | tf_op jit(solution)/shard_map/all_to_all | solution.py:303
  26.3 0.0 copy-done
  26.3 1.1 dispatch.1
  27.4 16.4 %all-to-all-start.4 = ((bf16[16,32,256]{2,1,0:T(8,128)(2,1)}), bf16[16,32,256]{2,1,0:T(8,128)(2,1)S(1)}, u32[]{:S(2)}, u32[]{:S(2)}) async-start(bf16[16,32,256]{2,1,0:T(8,128)(2,1)} %bitcast.15), calls=%async_computation.4 | async-start | bytes 524288 | tf_op jit(solution)/shard_map/all_to_all | solution.py:303
  43.8 15.0 %all-to-all-done.4 = bf16[16,32,256]{2,1,0:T(8,128)(2,1)S(1)} async-done(((bf16[16,32,256]{2,1,0:T(8,128)(2,1)}), bf16[16,32,256]{2,1,0:T(8,128)(2,1)S(1)}, u32[]{:S(2)}, u32[]{:S(2)}) %all-to-all-start.4) | async-done | bytes 262176 | tf_op jit(solution)/shard_map/all_to_all | solution.py:303
  58.8 0.7 slice_reduce_fusion
  60.2 0.0 copy-start.3
  60.2 2.0 %conditional.2 = ((bf16[8,4,96,256]{3,2,1,0:T(8,128)(2,1)}, f32[8,128]{1,0:T(8,128)S(1)})) conditional(s32[]{:T(128)} %convert_element_type.2, bf16[16,32,256]{2,1,0:T(8,128)(2,1)S(1)} %all-to-all-done.4, (s32[128,2]{0,1:T(2,128)S(1)}, bf16[128,256]{1,0:T(8,128)(2,1)S(1)}) %tuple.32), branch_computations={%region_1.0_spmd, %region_2.0_spmd} | conditional | flops 3000000 | bytes 3790556 | solution.py:395
  60.2 1.9 %spread.1 = (bf16[8,4,96,256]{3,2,1,0:T(8,128)(2,1)}, f32[8,128]{1,0:T(8,128)S(1)}) custom-call(bf16[512,256]{1,0:T(8,128)(2,1)S(1)} %bitcast.37), custom_call_target="tpu_custom_call" | custom-call | flops 1000000 | bytes 1000000 | tf_op jit(solution)/shard_map/cond/branch_0_fun/spread/pallas_call | solution.py:49
  62.1 27.8 %all_to_all.55 = bf16[32,96,256]{2,1,0:T(8,128)(2,1)S(1)} all-to-all(bf16[32,96,256]{2,1,0:T(8,128)(2,1)} %bitcast.36), channel_id=1, replica_groups=mesh['z'=16,'y'=4,'c'=2,'x'=4] {'y','c','x'}, dimensions={0} | all-to-all | bytes 3145728 | tf_op jit(solution)/shard_map/all_to_all | solution.py:303
  90.0 0.0 copy-done.3
  90.0 3.8 %experts.1 = bf16[8,4,96,256]{3,2,1,0:T(8,128)(2,1)S(1)} custom-call(bf16[8,4,96,256]{3,2,1,0:T(8,128)(2,1)S(1)} %bitcast.22, f32[1,1024]{1,0:T(1,128)S(1)} %bitcast.30, bf16[1024,1024]{1,0:T(8,128)(2,1)S(1)} %bitcast.31, bf16[1024,1024]{1,0:T(8,128)(2,1)S(1)} %bitcast.32), custom_call_target="tpu_custom_call" | custom-call | flops 3221225472 | bytes 8388608 | tf_op jit(solution)/shard_map/experts/pallas_call | solution.py:254
  93.8 26.8 %all_to_all.56 = bf16[32,96,256]{2,1,0:T(8,128)(2,1)S(1)} all-to-all(bf16[32,96,256]{2,1,0:T(8,128)(2,1)S(1)} %bitcast.23), channel_id=1, replica_groups=mesh['z'=16,'y'=4,'c'=2,'x'=4] {'y','c','x'}, dimensions={0} | all-to-all | bytes 3145728 | tf_op jit(solution)/shard_map/all_to_all | solution.py:303
  120.6 25.1 %conditional.3 = (bf16[128,256]{1,0:T(8,128)(2,1)S(1)}) conditional(s32[]{:T(128)} %convert_element_type.2, (bf16[8,4,96,256]{3,2,1,0:T(8,128)(2,1)S(1)}, f32[8,128]{1,0:T(8,128)S(1)}, bf16[2,128,512]{2,1,0:T(8,128)(2,1)S(1)}, f32[2,128,128]{2,1,0:T(8,128)S(1)}, f32[128,256]{1,0:T(8,128)S(1)}) %tuple.29, (bf16[8,4,96,256]{3,2,1,0:T(8,128)(2,1)S(1)}, ...), branch_computations={%region_3.0_spmd, %region_4.0_spmd} | conditional | flops 3000000 | bytes 4179688 | solution.py:418
  120.6 0.7 collect.1
  121.3 24.1 %all_to_all.54 = bf16[16,32,256]{2,1,0:T(8,128)(2,1)S(1)} all-to-all(bf16[16,32,256]{2,1,0:T(8,128)(2,1)S(1)} %bitcast.27), channel_id=1, replica_groups=mesh['z'=16,'y'=4,'c'=2,'x'=4] {'z'}, dimensions={0} | all-to-all | bytes 524288 | tf_op jit(solution)/shard_map/cond/branch_0_fun/all_to_all | solution.py:303
  145.4 0.2 combine.1
  145.7 0.0 copy-start.5
  145.7 0.6 copy-done.5
  (8 shorter events, 0.0 us)
Async XLA Ops:
  0.0 26.3 %copy-start = (bf16[128,1024]{1,0:T(8,128)(2,1)S(1)}, bf16[128,1024]{1,0:T(8,128)(2,1)}, u32[]{:S(2)}) copy-start(bf16[128,1024]{1,0:T(8,128)(2,1)} %input_ref.3) | copy-start | bytes 786436
  0.0 19.5 %copy-start.8 = (s32[128,2]{0,1:T(2,128)S(1)}, s32[128,2]{0,1:T(2,128)}, u32[]{:S(2)}) copy-start(s32[128,2]{0,1:T(2,128)} %param.24) | copy-start | bytes 3076
  0.0 19.5 %copy-start.4 = (f32[128,2]{0,1:T(2,128)S(1)}, f32[128,2]{0,1:T(2,128)}, u32[]{:S(2)}) copy-start(f32[128,2]{0,1:T(2,128)} %param.25) | copy-start | bytes 3076
  0.0 26.3 %copy-start.1 = (f32[1024]{0:T(1024)S(1)}, f32[1024]{0:T(1024)}, u32[]{:S(2)}) copy-start(f32[1024]{0:T(1024)} %param.21) | copy-start | bytes 12292
  0.0 8.0 %collective-permute-start.1 = (bf16[128,256]{1,0:T(8,128)(2,1)}, bf16[128,256]{1,0:T(8,128)(2,1)S(1)}, u32[]{:S(2)}, u32[]{:S(2)}) collective-permute-start(bf16[128,256]{1,0:T(8,128)(2,1)} %glu_ref.1), channel_id=1, source_target_pairs={{4,0},{8,4},{12,8},{16,12},{20,16},{24,20},{28,24},{32,28},{36,32}... | collective-permute-start | bytes 196616 | tf_op jit(solution)/shard_map/ppermute | solution.py:312
  4.1 7.9 %collective-permute-start = (bf16[128,256]{1,0:T(8,128)(2,1)}, bf16[128,256]{1,0:T(8,128)(2,1)S(1)}, u32[]{:S(2)}, u32[]{:S(2)}) collective-permute-start(bf16[128,256]{1,0:T(8,128)(2,1)} %glu_ref.1), channel_id=1, source_target_pairs={{0,4},{4,8},{8,12},{12,16},{16,20},{20,24},{24,28},{28,32},{32,36}... | collective-permute-start | bytes 196616 | tf_op jit(solution)/shard_map/ppermute | solution.py:311
  8.1 3.9 %copy-start.6 = (bf16[128,256]{1,0:T(8,128)(2,1)}, bf16[128,256]{1,0:T(8,128)(2,1)S(1)}, u32[]{:S(2)}) copy-start(bf16[128,256]{1,0:T(8,128)(2,1)S(1)} %collective-permute-done.1.high_ref) | copy-start | bytes 196612
  12.0 0.6 copy-start.7
  15.2 11.1 %all-to-all-start.3 = ((bf16[4,144,256]{2,1,0:T(8,128)(2,1)}), bf16[4,144,256]{2,1,0:T(8,128)(2,1)S(1)}, u32[]{:S(2)}, u32[]{:S(2)}) async-start(bf16[4,144,256]{2,1,0:T(8,128)(2,1)} %front.1), calls=%async_computation.3 | async-start | bytes 589824 | tf_op jit(solution)/shard_map/all_to_all | solution.py:303
  27.4 31.4 %all-to-all-start.4 = ((bf16[16,32,256]{2,1,0:T(8,128)(2,1)}), bf16[16,32,256]{2,1,0:T(8,128)(2,1)S(1)}, u32[]{:S(2)}, u32[]{:S(2)}) async-start(bf16[16,32,256]{2,1,0:T(8,128)(2,1)} %bitcast.15), calls=%async_computation.4 | async-start | bytes 524288 | tf_op jit(solution)/shard_map/all_to_all | solution.py:303
  60.2 29.8 %copy-start.3 = (bf16[1,1024,1024]{2,1,0:T(8,128)(2,1)S(1)}, bf16[1,1024,1024]{2,1,0:T(8,128)(2,1)}, u32[]{:S(2)}) copy-start(bf16[1,1024,1024]{2,1,0:T(8,128)(2,1)} %param.23) | copy-start | bytes 6291460
  62.1 27.8 %copy-start.2 = (bf16[1,1024,1024]{2,1,0:T(8,128)(2,1)S(1)}, bf16[1,1024,1024]{2,1,0:T(8,128)(2,1)}, u32[]{:S(2)}) copy-start(bf16[1,1024,1024]{2,1,0:T(8,128)(2,1)} %param.22) | copy-start | bytes 6291460
  145.7 0.6 copy-start.5

commit v4 on v3

--- a/solution.py
+++ b/solution.py
@@ -129,7 +129,7 @@
     counts_ref[...] = dot(last, values.astype(BF16)).astype(BF16)
 
 
-def own_conv_kernel(glu_ref, taps_ref, out_ref, padded):
+def own_conv_kernel(glu_ref, taps_ref, out_ref, same_ref, padded):
     padded[0:EDGE] = jnp.zeros((EDGE, QUARTER), F32)
     padded[EDGE + ROWS :] = jnp.zeros((EDGE, QUARTER), F32)
     padded[EDGE : EDGE + ROWS] = glu_ref[...].astype(F32)
@@ -138,15 +138,21 @@
         term = padded[k + 1 : k + 1 + ROWS] * taps_ref[k : k + 1]
         total = term if total is None else total + term
     out_ref[...] = total
+    same_ref[...] = glu_ref[...]
 
 
 def front_kernel(
-    own_ref, low_ref, high_ref, taps_ref, scale_ref, shift_ref, pw_ref, input_ref, out_ref, low, high, depth
+    core_ref, own_ref, beyond_ref, beside_ref, taps_ref, scale_ref, shift_ref, pw_ref, input_ref, out_ref, low, high, depth
 ):
-    low[0:EDGE] = low_ref[ROWS - EDGE :].astype(F32)
+    first_core = core_ref[0] == 0
+    tail = pl.ds(ROWS - EDGE, EDGE)
+    head = pl.ds(0, EDGE)
+    low[0:EDGE] = jnp.where(first_core, beyond_ref[tail].astype(F32), beside_ref[tail].astype(F32))
     low[EDGE:] = jnp.zeros((2 * EDGE, QUARTER), F32)
     high[0 : 2 * EDGE] = jnp.zeros((2 * EDGE, QUARTER), F32)
-    high[2 * EDGE :] = high_ref[0:EDGE].astype(F32)
+    high[2 * EDGE :] = jnp.where(
+        first_core, beside_ref[head].astype(F32), beyond_ref[head].astype(F32)
+    )
     depth[...] = own_ref[...]
     first, last = depth[0:EDGE], depth[ROWS - EDGE :]
     for k in range(TAPS):
@@ -190,10 +196,9 @@
     mixed_ref[...] = mixed
     scaled = ((mixed - mean) * gain_ref[:, columns]).astype(BF16)
     scaled_ref[...] = scaled
-    out_ref[...] = dot(put_ref[...], scaled).astype(BF16)
-    for z in range(Z):
-        tail = pl.ds(z * SHORT + SHORT - 16, 16)
-        out_ref[tail, 0:ROWS] = out_ref[tail, 0:ROWS] + counts_ref[tail]
+    sent = dot(put_ref[...], scaled)
+    out_ref[:, 0:ROWS] = (sent[:, 0:ROWS] + counts_ref[...].astype(F32)).astype(BF16)
+    out_ref[:, ROWS:] = sent[:, ROWS:].astype(BF16)
 
 
 def full_dispatch_kernel(scaled_ref, put_ref, out_ref):
@@ -215,6 +220,8 @@
     wide[...] = rows[:, 0:ROWS].astype(F32)
     lane = lax.broadcasted_iota(jnp.int32, (Z, ROWS), 1)
     counts = wide[pl.ds(SHORT - 1, Z, stride=SHORT)]
+    crowded = jnp.max(jnp.where(lane == YC, counts, 0.0), axis=(0, 1), keepdims=True) > 0.5
+    mark = jnp.where(crowded, jnp.inf, 0.0)
     counts = jnp.where(lane < YC, counts, 0.0).astype(BF16)
     lower = lax.broadcasted_iota(jnp.int32, (ROWS, ROWS), 0)
     upper = lax.broadcasted_iota(jnp.int32, (ROWS, ROWS), 1)
@@ -225,23 +232,41 @@
     position = (row % CAP).astype(F32)
     source = (row // CAP * SHORT).astype(F32) + dot(sender, starts) + position
     source = jnp.where(position < dot(sender, counts), source, -1.0)
-    packed = lax.broadcasted_iota(jnp.int32, (BLOCK, PACKED), 1).astype(F32)
-    for yc in range(YC):
-        take = (packed == source[:, yc : yc + 1]).astype(F32).astype(BF16)
-        block = dot(take, rows).astype(BF16)
-        for x in range(X):
-            out_ref[yc, x] = block
+    rows_half, block_half = PACKED // 2, BLOCK // 2
+    packed = lax.broadcasted_iota(jnp.int32, (block_half, rows_half), 1).astype(F32)
+    for half in range(2):
+        mine = pl.ds(half * block_half, block_half)
+        wanted = source[half * block_half : (half + 1) * block_half] - float(half * rows_half)
+        take = jnp.concatenate(
+            [(packed == wanted[:, yc : yc + 1]).astype(F32).astype(BF16) for yc in range(YC)],
+            axis=0,
+        )
+        blocks = dot(take, rows[half * rows_half : (half + 1) * rows_half])
+        blocks = (blocks + mark).astype(BF16)
+        for yc in range(YC):
+            for x in range(X):
+                out_ref[yc, x, mine] = blocks[yc * block_half : (yc + 1) * block_half]
     source = jnp.concatenate([source, jnp.full((ROWS - BLOCK, ROWS), -1.0, F32)], axis=0)
     source_ref[...] = jnp.transpose(source)[0:YC]
 
 
-def expert_kernel(in_ref, gain_ref, up_ref, down_ref, out_ref):
+def expert_kernel(in_ref, gain_ref, up_ref, down_ref, out_ref, mark_ref):
     blocks = in_ref.shape[0]
     rows = jnp.concatenate(
         [in_ref[:, x].reshape(blocks * BLOCK, QUARTER) for x in range(X)], axis=1
     )
-    centered = rows.astype(F32) / gain_ref[...]
+    centered = rows.astype(F32) * (1.0 / gain_ref[...])
     spread = jnp.sum(centered * centered, axis=1, keepdims=True) * (1.0 / WIDTH)
+    marked = jnp.where(jnp.max(spread) == jnp.inf, 1, 0)
+
+    @pl.when(pl.program_id(0) == 0)
+    def _():
+        mark_ref[0] = marked
+
+    @pl.when(pl.program_id(0) > 0)
+    def _():
+        mark_ref[0] = jnp.maximum(mark_ref[0], marked)
+
     inverse = 1.0 / jnp.sqrt(spread + 1e-05)
     hidden = silu(dot(rows, up_ref[...]) * inverse).astype(BF16)
     result = dot(hidden, down_ref[...]).astype(BF16)
@@ -254,14 +279,17 @@
     return pl.pallas_call(
         expert_kernel,
         grid=(YC // step,),
-        out_shape=shape((YC, X, BLOCK, QUARTER), BF16),
+        out_shape=(shape((YC, X, BLOCK, QUARTER), BF16), shape((1,), jnp.int32)),
         in_specs=[
             pl.BlockSpec((step, X, BLOCK, QUARTER), lambda i: (i, 0, 0, 0)),
             pl.BlockSpec((1, WIDTH), lambda i: (0, 0)),
             pl.BlockSpec((WIDTH, WIDTH), lambda i: (0, 0)),
             pl.BlockSpec((WIDTH, WIDTH), lambda i: (0, 0)),
         ],
-        out_specs=pl.BlockSpec((step, X, BLOCK, QUARTER), lambda i: (i, 0, 0, 0)),
+        out_specs=(
+            pl.BlockSpec((step, X, BLOCK, QUARTER), lambda i: (i, 0, 0, 0)),
+            pl.BlockSpec(memory_space=pltpu.SMEM),
+        ),
         cost_estimate=cost(4 * YC * BLOCK * WIDTH * WIDTH, 8 << 20),
         compiler_params=pltpu.CompilerParams(vmem_limit_bytes=40 << 20),
         name="experts",
@@ -303,13 +331,30 @@
     return lax.all_to_all(value, axes, split_axis=0, concat_axis=0, tiled=True)
 
 
+def through_experts(rows, gain, w_up, w_down):
+    rows = exchange(rows.reshape(YC * X, BLOCK, QUARTER), ("y", "c", "x"))
+    rows, marked = experts(rows.reshape(YC, X, BLOCK, QUARTER), gain, w_up[0], w_down[0])
+    rows = exchange(rows.reshape(YC * X, BLOCK, QUARTER), ("y", "c", "x"))
+    return rows.reshape(YC, X, BLOCK, QUARTER), marked
+
+
 def on_device(
     glu, dw_kernel, bn_scale, bn_shift, pw_out, block_input, ln_gain, w_up, w_down, routes, gates
 ):
     seq = ("z", "y", "c")
     count = Z * Y * C
-    low = lax.ppermute(glu, seq, [(i, i + 1) for i in range(count - 1)])
-    high = lax.ppermute(glu, seq, [(i + 1, i) for i in range(count - 1)])
+    pairs = [(i, i + 1) for i in range(1, count - 1, 2)]
+    beyond = lax.ppermute(glu, seq, pairs + [(j, i) for i, j in pairs])
+    own, same = call(
+        own_conv_kernel,
+        (shape((ROWS, QUARTER), F32), shape((ROWS, QUARTER), BF16)),
+        "own_conv",
+        vmem=60 << 20,
+        scratch=[pltpu.VMEM((ROWS + 2 * EDGE, QUARTER), F32)],
+    )(glu, dw_kernel)
+    pairs = [(i, i + 1) for i in range(0, count, 2)]
+    beside = lax.ppermute(same, seq, pairs + [(j, i) for i, j in pairs])
+    core = lax.axis_index("c").astype(jnp.int32).reshape(1)
     gain = ln_gain.reshape(1, WIDTH)
     hid_index = lax.axis_index("x").astype(jnp.int32).reshape(1)
 
@@ -323,27 +368,22 @@
         ),
         "routing",
     )(routes.T, gates.T)
-    own = call(
-        own_conv_kernel,
-        shape((ROWS, QUARTER), F32),
-        "own_conv",
-        vmem=60 << 20,
-        scratch=[pltpu.VMEM((ROWS + 2 * EDGE, QUARTER), F32)],
-    )(glu, dw_kernel)
     parts = call(
         front_kernel,
         shape((X, ROWS + AUX, QUARTER), BF16),
         "front",
         vmem=60 << 20,
+        smem=(0,),
         scratch=[
             pltpu.VMEM((3 * EDGE, QUARTER), F32),
             pltpu.VMEM((3 * EDGE, QUARTER), F32),
             pltpu.VMEM((ROWS, QUARTER), F32),
         ],
     )(
+        core,
         own,
-        low,
-        high,
+        beyond,
+        beside,
         dw_kernel,
         bn_scale.reshape(1, QUARTER),
         bn_shift.reshape(1, QUARTER),
@@ -362,60 +402,46 @@
         smem=(0,),
     )(hid_index, parts, block_input, gain, put, counts)
     rows = exchange(rows, "z")
-    flags = rows.reshape(Z, SHORT, QUARTER)[:, SHORT - 1, YC]
-    crowded = jnp.max(flags.astype(F32)) > 0.5
-
-    def full_slots():
-        return call(
+    rows, source = call(
+        spread_kernel,
+        (shape((YC, X, BLOCK, QUARTER), BF16), shape((YC, ROWS), F32)),
+        "spread",
+        scratch=[pltpu.VMEM((PACKED, ROWS), F32)],
+    )(rows)
+    rows, marked = through_experts(rows, gain, w_up, w_down)
+    rows = call(collect_kernel, shape((PACKED, QUARTER), BF16), "collect")(rows, source)
+    rows = exchange(rows, "z")
+
+    def short(rows):
+        return call(combine_kernel, shape((ROWS, QUARTER), BF16), "combine")(
+            rows, pick, gate, mixed
+        )
+
+    def full(_):
+        put, pick = call(
             full_routing_kernel,
             (shape((SLOTS, ROWS), BF16), shape((2, ROWS, SLOTS), BF16)),
             "full_routing",
         )(routes.T)
-
-    def full_out(_):
-        sent = call(full_dispatch_kernel, shape((SLOTS, QUARTER), BF16), "full_dispatch")(
-            scaled, full_slots()[0]
-        )
-        blocks = call(
+        rows = call(full_dispatch_kernel, shape((SLOTS, QUARTER), BF16), "full_dispatch")(scaled, put)
+        rows = call(
             full_spread_kernel,
             shape((YC, X, BLOCK, QUARTER), BF16),
             "full_spread",
             scratch=[pltpu.VMEM((2, SLOTS, 128), F32)],
-        )(exchange(sent, "z"))
-        return blocks, jnp.zeros((YC, ROWS), F32)
-
-    def short_out(packed):
-        return call(
-            spread_kernel,
-            (shape((YC, X, BLOCK, QUARTER), BF16), shape((YC, ROWS), F32)),
-            "spread",
-            scratch=[pltpu.VMEM((PACKED, ROWS), F32)],
-        )(packed)
-
-    rows, source = lax.cond(crowded, full_out, short_out, rows)
-    rows = exchange(rows.reshape(YC * X, BLOCK, QUARTER), ("y", "c", "x"))
-    rows = experts(rows.reshape(YC, X, BLOCK, QUARTER), gain, w_up[0], w_down[0])
-    rows = exchange(rows.reshape(YC * X, BLOCK, QUARTER), ("y", "c", "x"))
-    rows = rows.reshape(YC, X, BLOCK, QUARTER)
-
-    def full_back(blocks):
-        sent = call(
+        )(exchange(rows, "z"))
+        rows, _ = through_experts(rows, gain, w_up, w_down)
+        rows = call(
             full_collect_kernel,
             shape((SLOTS, QUARTER), BF16),
             "full_collect",
             scratch=[pltpu.VMEM((2, SLOTS, 128), F32)],
-        )(blocks)
+        )(rows)
         return call(combine_kernel, shape((ROWS, QUARTER), BF16), "full_combine")(
-            exchange(sent, "z"), full_slots()[1], gate, mixed
+            exchange(rows, "z"), pick, gate, mixed
         )
 
-    def short_back(blocks):
-        sent = call(collect_kernel, shape((PACKED, QUARTER), BF16), "collect")(blocks, source)
-        return call(combine_kernel, shape((ROWS, QUARTER), BF16), "combine")(
-            exchange(sent, "z"), pick, gate, mixed
-        )
-
-    return lax.cond(crowded, full_back, short_back, rows)
+    return lax.cond(marked[0] > 0, full, short, rows)
 
 
 def solution(mesh):

time: 147 us -> 143 us (0.973)
  starting transfers between devices: 26.7 us -> 15.8 us
  blocking collectives: 78.7 us -> 87.2 us
    all_to_all x2, starting transfers between devices: 20.7 us -> 9.88 us  [exchange(): return lax.all_to_all(value, axes, split_axis=0, concat_axis=0, tiled=True)]
    all_to_all x3, blocking collectives: 78.7 us -> 87.2 us  [exchange(): return lax.all_to_all(value, axes, split_axis=0, concat_axis=0, tiled=True)]
    all_to_all x2, waiting for transfers between devices: 21.2 us -> 24.2 us  [exchange(): return lax.all_to_all(value, axes, split_axis=0, concat_axis=0, tiled=True)]
    ppermute x2, waiting for transfers between devices: 3.91 us -> 1.41 us  [the longest x1 1.4 us: on_device(): beside = lax.ppermute(same, seq, pairs + [(j, i) for i, j in pairs])]
where the time goes in v4:
time: 143 us
  blocking collectives  87.2 us (61%)
  waiting for transfers between devices  25.6 us (18%)
  starting transfers between devices  15.8 us (11%)
  Pallas kernels  11.9 us (8%)
    all_to_all x3, blocking collectives, exchange(): return lax.all_to_all(value, axes, split_axis=0, concat_axis=0, tiled=True)  87.2 us
    all_to_all x2, waiting for transfers between devices, exchange(): return lax.all_to_all(value, axes, split_axis=0, concat_axis=0, tiled=True)  24.2 us
    all_to_all x2, starting transfers between devices, exchange(): return lax.all_to_all(value, axes, split_axis=0, concat_axis=0, tiled=True)  9.88 us
    pallas_call x7, Pallas kernels, run(): pl.pallas_call(body, grid=(1,), out_shape=out_shape, in_specs=in_specs, o...  7.94 us
    ppermute x1, starting transfers between devices, on_device(): beyond = lax.ppermute(glu, seq, pairs + [(j, i) for i, j in pairs])  4.04 us
    pallas_call x1, Pallas kernels, experts(): pl.pallas_call(expert_kernel, grid=(YC // step,), out_shape=(shape((YC, X...  4 us
  transfers between devices with their start and end apart: 4, of which 3 were waited for; matrix products, arithmetic and copies ran while one was open for 0% of the time, Pallas kernels for 2%

profile of v4, /device:TPU:32, one launch (start us, length us, event | category | flops | bytes accessed | tf_op | source)
XLA Modules:
  0.0 142.6 jit_solution(10614778851921351290)
XLA Ops:
  0.0 0.0 copy-start.5
  0.0 4.0 %collective-permute-start = (bf16[128,256]{1,0:T(8,128)(2,1)}, bf16[128,256]{1,0:T(8,128)(2,1)S(1)}, u32[]{:S(2)}, u32[]{:S(2)}) collective-permute-start(bf16[128,256]{1,0:T(8,128)(2,1)} %glu_ref.1), channel_id=1, source_target_pairs={{4,8},{12,16},{20,24},{28,32},{36,40},{44,48},{52,56},{60,64},{68,... | collective-permute-start | bytes 196616 | tf_op jit(solution)/shard_map/ppermute | solution.py:347
  4.1 2.1 %own_conv.1 = (f32[128,256]{1,0:T(8,128)}, bf16[128,256]{1,0:T(8,128)(2,1)}) custom-call(bf16[128,256]{1,0:T(8,128)(2,1)} %glu_ref.1, f32[31,256]{1,0:T(8,128)} %taps_ref.3), custom_call_target="tpu_custom_call" | custom-call | flops 1000000 | bytes 1000000 | tf_op jit(solution)/shard_map/own_conv/pallas_call | solution.py:49
  6.1 1.9 %collective-permute-start.1 = (bf16[128,256]{1,0:T(8,128)(2,1)}, bf16[128,256]{1,0:T(8,128)(2,1)S(1)}, u32[]{:S(2)}, u32[]{:S(2)}) collective-permute-start(bf16[128,256]{1,0:T(8,128)(2,1)} %get-tuple-element.59), channel_id=1, source_target_pairs={{0,4},{8,12},{16,20},{24,28},{32,36},{40,44},{48,52},{56,60},{64,6... | collective-permute-start | bytes 196616 | tf_op jit(solution)/shard_map/ppermute | solution.py:356
  8.1 0.0 collective-permute-done.beyond_ref
  8.1 0.0 copy-start.2
  8.1 1.4 collective-permute-done.1.beside_ref
  9.5 0.0 copy-done.2
  9.5 0.6 copy-done.3
  10.1 2.6 %front.1 = bf16[4,144,256]{2,1,0:T(8,128)(2,1)} custom-call(s32[1]{0:T(128)} %bitcast.13.core_ref, f32[128,256]{1,0:T(8,128)} %get-tuple-element.58.own_ref, bf16[128,256]{1,0:T(8,128)(2,1)} %copy-done.2, bf16[128,256]{1,0:T(8,128)(2,1)} %copy-done.3, f32[31,256]{1,0:T(8,128)} %taps_ref.3, f32[1,256]{1,0:T(1,128)} %bitcast.48, f32[1,256]{1,0:T(1,128)} %bitcast.49, ...), custom_call_target="tpu_custom_call" | custom-call | flops 1000000 | bytes 1000000 | tf_op jit(solution)/shard_map/front/pallas_call | solution.py:49
  12.7 4.3 %all-to-all-start.4 = ((bf16[4,144,256]{2,1,0:T(8,128)(2,1)}), bf16[4,144,256]{2,1,0:T(8,128)(2,1)S(1)}, u32[]{:S(2)}, u32[]{:S(2)}) async-start(bf16[4,144,256]{2,1,0:T(8,128)(2,1)} %front.1), calls=%async_computation.4 | async-start | bytes 589824 | tf_op jit(solution)/shard_map/all_to_all | solution.py:331
  17.0 0.0 copy-done.9
  17.0 0.0 copy-done.1
  17.0 0.6 routing.1
  17.6 6.7 %all-to-all-done.4.parts_ref = bf16[4,144,256]{2,1,0:T(8,128)(2,1)S(1)} async-done(((bf16[4,144,256]{2,1,0:T(8,128)(2,1)}), bf16[4,144,256]{2,1,0:T(8,128)(2,1)S(1)}, u32[]{:S(2)}, u32[]{:S(2)}) %all-to-all-start.4) | async-done | bytes 294944 | tf_op jit(solution)/shard_map/all_to_all | solution.py:331
  24.3 0.0 copy-done
  24.3 0.0 copy-done.5
  24.3 0.4 dispatch.1
  24.7 33.1 %all_to_all.65 = bf16[16,32,256]{2,1,0:T(8,128)(2,1)S(1)} all-to-all(bf16[16,32,256]{2,1,0:T(8,128)(2,1)S(1)} %bitcast.42), channel_id=1, replica_groups=mesh['z'=16,'y'=4,'c'=2,'x'=4] {'z'}, dimensions={0} | all-to-all | bytes 524288 | tf_op jit(solution)/shard_map/all_to_all | solution.py:331
  57.8 0.7 spread.1
  58.5 0.0 copy-start.6
  58.5 27.3 %all_to_all.66 = bf16[32,96,256]{2,1,0:T(8,128)(2,1)S(1)} all-to-all(bf16[32,96,256]{2,1,0:T(8,128)(2,1)S(1)} %bitcast.32), channel_id=1, replica_groups=mesh['z'=16,'y'=4,'c'=2,'x'=4] {'y','c','x'}, dimensions={0} | all-to-all | bytes 3145728 | tf_op jit(solution)/shard_map/all_to_all | solution.py:331
  85.8 0.0 copy-done.7
  85.8 4.0 %experts.3 = (bf16[8,4,96,256]{3,2,1,0:T(8,128)(2,1)S(1)}, s32[1]{0:T(128)}) custom-call(bf16[8,4,96,256]{3,2,1,0:T(8,128)(2,1)S(1)} %bitcast.33, f32[1,1024]{1,0:T(1,128)S(1)} %bitcast.46, bf16[1024,1024]{1,0:T(8,128)(2,1)S(1)} %bitcast.50, bf16[1024,1024]{1,0:T(8,128)(2,1)S(1)} %bitcast.52), custom_call_target="tpu_custom_call" | custom-call | flops 3221225472 | bytes 8388608 | tf_op jit(solution)/shard_map/experts/pallas_call | solution.py:279
  89.8 26.8 %all_to_all.67 = bf16[32,96,256]{2,1,0:T(8,128)(2,1)S(1)} all-to-all(bf16[32,96,256]{2,1,0:T(8,128)(2,1)S(1)} %bitcast.34), channel_id=1, replica_groups=mesh['z'=16,'y'=4,'c'=2,'x'=4] {'y','c','x'}, dimensions={0} | all-to-all | bytes 3145728 | tf_op jit(solution)/shard_map/all_to_all | solution.py:331
  116.6 1.4 %collect.1 = bf16[512,256]{1,0:T(8,128)(2,1)} custom-call(bf16[8,4,96,256]{3,2,1,0:T(8,128)(2,1)S(1)} %bitcast.29, f32[8,128]{1,0:T(8,128)S(1)} %get-tuple-element.66.source_ref), custom_call_target="tpu_custom_call" | custom-call | flops 1000000 | bytes 1000000 | tf_op jit(solution)/shard_map/collect/pallas_call | solution.py:49
  118.0 5.6 %all-to-all-start.8 = ((bf16[16,32,256]{2,1,0:T(8,128)(2,1)}), bf16[16,32,256]{2,1,0:T(8,128)(2,1)S(1)}, u32[]{:S(2)}, u32[]{:S(2)}) async-start(bf16[16,32,256]{2,1,0:T(8,128)(2,1)} %bitcast.28), calls=%async_computation.8 | async-start | bytes 524288 | tf_op jit(solution)/shard_map/all_to_all | solution.py:331
  124.3 17.5 %all-to-all-done.8 = bf16[16,32,256]{2,1,0:T(8,128)(2,1)S(1)} async-done(((bf16[16,32,256]{2,1,0:T(8,128)(2,1)}), bf16[16,32,256]{2,1,0:T(8,128)(2,1)S(1)}, u32[]{:S(2)}, u32[]{:S(2)}) %all-to-all-start.8) | async-done | bytes 262176 | tf_op jit(solution)/shard_map/all_to_all | solution.py:331
  141.8 0.2 conditional.1
  141.8 0.2 combine.1
  142.0 0.0 copy-start.4
  142.0 0.6 copy-done.4
  (6 shorter events, 0.0 us)
Async XLA Ops:
  0.0 24.3 %copy-start = (bf16[128,1024]{1,0:T(8,128)(2,1)S(1)}, bf16[128,1024]{1,0:T(8,128)(2,1)}, u32[]{:S(2)}) copy-start(bf16[128,1024]{1,0:T(8,128)(2,1)} %input_ref.3) | copy-start | bytes 786436
  0.0 17.0 %copy-start.9 = (s32[128,2]{0,1:T(2,128)S(1)}, s32[128,2]{0,1:T(2,128)}, u32[]{:S(2)}) copy-start(s32[128,2]{0,1:T(2,128)} %param.22) | copy-start | bytes 3076
  0.0 17.0 %copy-start.1 = (f32[128,2]{0,1:T(2,128)S(1)}, f32[128,2]{0,1:T(2,128)}, u32[]{:S(2)}) copy-start(f32[128,2]{0,1:T(2,128)} %param.23) | copy-start | bytes 3076
  0.0 24.3 %copy-start.5 = (f32[1024]{0:T(1024)S(1)}, f32[1024]{0:T(1024)}, u32[]{:S(2)}) copy-start(f32[1024]{0:T(1024)} %param.19) | copy-start | bytes 12292
  0.0 8.0 %collective-permute-start = (bf16[128,256]{1,0:T(8,128)(2,1)}, bf16[128,256]{1,0:T(8,128)(2,1)S(1)}, u32[]{:S(2)}, u32[]{:S(2)}) collective-permute-start(bf16[128,256]{1,0:T(8,128)(2,1)} %glu_ref.1), channel_id=1, source_target_pairs={{4,8},{12,16},{20,24},{28,32},{36,40},{44,48},{52,56},{60,64},{68,... | collective-permute-start | bytes 196616 | tf_op jit(solution)/shard_map/ppermute | solution.py:347
  6.1 3.3 %collective-permute-start.1 = (bf16[128,256]{1,0:T(8,128)(2,1)}, bf16[128,256]{1,0:T(8,128)(2,1)S(1)}, u32[]{:S(2)}, u32[]{:S(2)}) collective-permute-start(bf16[128,256]{1,0:T(8,128)(2,1)} %get-tuple-element.59), channel_id=1, source_target_pairs={{0,4},{8,12},{16,20},{24,28},{32,36},{40,44},{48,52},{56,60},{64,6... | collective-permute-start | bytes 196616 | tf_op jit(solution)/shard_map/ppermute | solution.py:356
  8.1 1.4 copy-start.2
  9.5 0.6 copy-start.3
  12.7 11.6 %all-to-all-start.4 = ((bf16[4,144,256]{2,1,0:T(8,128)(2,1)}), bf16[4,144,256]{2,1,0:T(8,128)(2,1)S(1)}, u32[]{:S(2)}, u32[]{:S(2)}) async-start(bf16[4,144,256]{2,1,0:T(8,128)(2,1)} %front.1), calls=%async_computation.4 | async-start | bytes 589824 | tf_op jit(solution)/shard_map/all_to_all | solution.py:331
  24.3 61.5 %copy-start.7 = (bf16[1,1024,1024]{2,1,0:T(8,128)(2,1)S(1)}, bf16[1,1024,1024]{2,1,0:T(8,128)(2,1)}, u32[]{:S(2)}) copy-start(bf16[1,1024,1024]{2,1,0:T(8,128)(2,1)} %param.21) | copy-start | bytes 6291460
  58.5 27.3 %copy-start.6 = (bf16[1,1024,1024]{2,1,0:T(8,128)(2,1)S(1)}, bf16[1,1024,1024]{2,1,0:T(8,128)(2,1)}, u32[]{:S(2)}) copy-start(bf16[1,1024,1024]{2,1,0:T(8,128)(2,1)} %param.20) | copy-start | bytes 6291460
  118.0 23.7 %all-to-all-start.8 = ((bf16[16,32,256]{2,1,0:T(8,128)(2,1)}), bf16[16,32,256]{2,1,0:T(8,128)(2,1)S(1)}, u32[]{:S(2)}, u32[]{:S(2)}) async-start(bf16[16,32,256]{2,1,0:T(8,128)(2,1)} %bitcast.28), calls=%async_computation.8 | async-start | bytes 524288 | tf_op jit(solution)/shard_map/all_to_all | solution.py:331
  142.0 0.6 copy-start.4

commit v5 on v4

--- a/solution.py
+++ b/solution.py
@@ -129,7 +129,14 @@
     counts_ref[...] = dot(last, values.astype(BF16)).astype(BF16)
 
 
-def own_conv_kernel(glu_ref, taps_ref, out_ref, same_ref, padded):
+def edge_kernel(core_ref, glu_ref, out_ref):
+    first_core = core_ref[0] == 0
+    tail = glu_ref[ROWS - EDGE :].astype(F32)
+    head = glu_ref[0:EDGE].astype(F32)
+    out_ref[...] = jnp.where(first_core, tail, head).astype(BF16)
+
+
+def own_conv_kernel(glu_ref, taps_ref, out_ref, padded):
     padded[0:EDGE] = jnp.zeros((EDGE, QUARTER), F32)
     padded[EDGE + ROWS :] = jnp.zeros((EDGE, QUARTER), F32)
     padded[EDGE : EDGE + ROWS] = glu_ref[...].astype(F32)
@@ -138,7 +145,6 @@
         term = padded[k + 1 : k + 1 + ROWS] * taps_ref[k : k + 1]
         total = term if total is None else total + term
     out_ref[...] = total
-    same_ref[...] = glu_ref[...]
 
 
 def front_kernel(
@@ -147,11 +153,11 @@
     first_core = core_ref[0] == 0
     tail = pl.ds(ROWS - EDGE, EDGE)
     head = pl.ds(0, EDGE)
-    low[0:EDGE] = jnp.where(first_core, beyond_ref[tail].astype(F32), beside_ref[tail].astype(F32))
+    low[0:EDGE] = jnp.where(first_core, beyond_ref[tail].astype(F32), beside_ref[...].astype(F32))
     low[EDGE:] = jnp.zeros((2 * EDGE, QUARTER), F32)
     high[0 : 2 * EDGE] = jnp.zeros((2 * EDGE, QUARTER), F32)
     high[2 * EDGE :] = jnp.where(
-        first_core, beside_ref[head].astype(F32), beyond_ref[head].astype(F32)
+        first_core, beside_ref[...].astype(F32), beyond_ref[head].astype(F32)
     )
     depth[...] = own_ref[...]
     first, last = depth[0:EDGE], depth[ROWS - EDGE :]
@@ -345,16 +351,17 @@
     count = Z * Y * C
     pairs = [(i, i + 1) for i in range(1, count - 1, 2)]
     beyond = lax.ppermute(glu, seq, pairs + [(j, i) for i, j in pairs])
-    own, same = call(
+    own = call(
         own_conv_kernel,
-        (shape((ROWS, QUARTER), F32), shape((ROWS, QUARTER), BF16)),
+        shape((ROWS, QUARTER), F32),
         "own_conv",
         vmem=60 << 20,
         scratch=[pltpu.VMEM((ROWS + 2 * EDGE, QUARTER), F32)],
     )(glu, dw_kernel)
+    core = lax.axis_index("c").astype(jnp.int32).reshape(1)
+    edge = call(edge_kernel, shape((EDGE, QUARTER), BF16), "edge", vmem=60 << 20, smem=(0,))(core, glu)
     pairs = [(i, i + 1) for i in range(0, count, 2)]
-    beside = lax.ppermute(same, seq, pairs + [(j, i) for i, j in pairs])
-    core = lax.axis_index("c").astype(jnp.int32).reshape(1)
+    beside = lax.ppermute(edge, seq, pairs + [(j, i) for i, j in pairs])
     gain = ln_gain.reshape(1, WIDTH)
     hid_index = lax.axis_index("x").astype(jnp.int32).reshape(1)
 

time: 143 us -> 143 us (level)
  Pallas kernels: 11.9 us -> 13.4 us
    pallas_call x7 -> x8, Pallas kernels: 7.94 us -> 9.4 us  [run(): pl.pallas_call(body, grid=(1,), out_shape=out_shape, in_specs=in_specs, o...]
  transfers between devices with their start and end apart: 4 -> 4, of which waited for: 3 -> 2; matrix products, arithmetic and copies ran while one was open for 0% -> 0% of each run, Pallas kernels for 2% -> 3%
where the time goes in v5:
time: 143 us; the launch traced here: 142 us
  blocking collectives  86.8 us (61%)
  waiting for transfers between devices  24.6 us (17%)
  starting transfers between devices  15.6 us (11%)
  Pallas kernels  13.4 us (9%)
    all_to_all x3, blocking collectives, exchange(): return lax.all_to_all(value, axes, split_axis=0, concat_axis=0, tiled=True)  86.8 us
    all_to_all x2, waiting for transfers between devices, exchange(): return lax.all_to_all(value, axes, split_axis=0, concat_axis=0, tiled=True)  24.6 us
    all_to_all x2, starting transfers between devices, exchange(): return lax.all_to_all(value, axes, split_axis=0, concat_axis=0, tiled=True)  9.62 us
    pallas_call x8, Pallas kernels, run(): pl.pallas_call(body, grid=(1,), out_shape=out_shape, in_specs=in_specs, o...  9.4 us
    ppermute x1, starting transfers between devices, on_device(): beyond = lax.ppermute(glu, seq, pairs + [(j, i) for i, j in pairs])  4.04 us
    pallas_call x1, Pallas kernels, experts(): pl.pallas_call(expert_kernel, grid=(YC // step,), out_shape=(shape((YC, X...  4 us
  transfers between devices with their start and end apart: 4, of which 2 were waited for; matrix products, arithmetic and copies ran while one was open for 0% of the time, Pallas kernels for 3%

profile of v5, /device:TPU:32, one launch (start us, length us, event | category | flops | bytes accessed | tf_op | source)
XLA Modules:
  0.0 142.4 jit_solution(8425485463632173842)
XLA Ops:
  0.0 0.0 copy-start.5
  0.0 4.0 %collective-permute-start = (bf16[128,256]{1,0:T(8,128)(2,1)}, bf16[128,256]{1,0:T(8,128)(2,1)S(1)}, u32[]{:S(2)}, u32[]{:S(2)}) collective-permute-start(bf16[128,256]{1,0:T(8,128)(2,1)} %glu_ref.3), channel_id=1, source_target_pairs={{4,8},{12,16},{20,24},{28,32},{36,40},{44,48},{52,56},{60,64},{68,... | collective-permute-start | bytes 196616 | tf_op jit(solution)/shard_map/ppermute | solution.py:353
  4.1 1.4 %edge.1 = bf16[16,256]{1,0:T(8,128)(2,1)} custom-call(s32[1]{0:T(128)} %bitcast.13.core_ref, bf16[128,256]{1,0:T(8,128)(2,1)} %glu_ref.3), custom_call_target="tpu_custom_call" | custom-call | flops 1000000 | bytes 1000000 | tf_op jit(solution)/shard_map/edge/pallas_call | solution.py:49
  5.5 1.9 %collective-permute-start.1 = (bf16[16,256]{1,0:T(8,128)(2,1)}, bf16[16,256]{1,0:T(8,128)(2,1)S(1)}, u32[]{:S(2)}, u32[]{:S(2)}) collective-permute-start(bf16[16,256]{1,0:T(8,128)(2,1)} %edge.1), channel_id=1, source_target_pairs={{0,4},{8,12},{16,20},{24,28},{32,36},{40,44},{48,52},{56,60},{64,6... | collective-permute-start | bytes 24584 | tf_op jit(solution)/shard_map/ppermute | solution.py:364
  7.4 2.1 %own_conv.1.own_ref = f32[128,256]{1,0:T(8,128)} custom-call(bf16[128,256]{1,0:T(8,128)(2,1)} %glu_ref.3, f32[31,256]{1,0:T(8,128)} %taps_ref.3), custom_call_target="tpu_custom_call" | custom-call | flops 1000000 | bytes 1000000 | tf_op jit(solution)/shard_map/own_conv/pallas_call | solution.py:49
  9.5 0.0 collective-permute-done.1.beside_ref
  9.5 0.0 collective-permute-done.beyond_ref
  9.5 0.0 copy-start.2
  9.5 0.6 copy-done.4
  10.1 0.0 copy-done.2
  10.1 2.5 %front.1 = bf16[4,144,256]{2,1,0:T(8,128)(2,1)} custom-call(s32[1]{0:T(128)} %bitcast.13.core_ref, f32[128,256]{1,0:T(8,128)} %own_conv.1.own_ref, bf16[128,256]{1,0:T(8,128)(2,1)} %copy-done.2, bf16[16,256]{1,0:T(8,128)(2,1)} %copy-done.4, f32[31,256]{1,0:T(8,128)} %taps_ref.3, f32[1,256]{1,0:T(1,128)} %bitcast.48, f32[1,256]{1,0:T(1,128)} %bitcast.49, ...), custom_call_target="tpu_custom_call" | custom-call | flops 1000000 | bytes 1000000 | tf_op jit(solution)/shard_map/front/pallas_call | solution.py:49
  12.7 4.3 %all-to-all-start.4 = ((bf16[4,144,256]{2,1,0:T(8,128)(2,1)}), bf16[4,144,256]{2,1,0:T(8,128)(2,1)S(1)}, u32[]{:S(2)}, u32[]{:S(2)}) async-start(bf16[4,144,256]{2,1,0:T(8,128)(2,1)} %front.1), calls=%async_computation.4 | async-start | bytes 589824 | tf_op jit(solution)/shard_map/all_to_all | solution.py:337
  17.0 0.0 copy-done.9
  17.0 0.0 copy-done.1
  17.0 0.6 routing.1
  17.6 7.1 %all-to-all-done.4.parts_ref = bf16[4,144,256]{2,1,0:T(8,128)(2,1)S(1)} async-done(((bf16[4,144,256]{2,1,0:T(8,128)(2,1)}), bf16[4,144,256]{2,1,0:T(8,128)(2,1)S(1)}, u32[]{:S(2)}, u32[]{:S(2)}) %all-to-all-start.4) | async-done | bytes 294944 | tf_op jit(solution)/shard_map/all_to_all | solution.py:337
  24.7 0.0 copy-done
  24.7 0.0 copy-done.5
  24.7 0.4 dispatch.1
  25.1 32.9 %all_to_all.65 = bf16[16,32,256]{2,1,0:T(8,128)(2,1)S(1)} all-to-all(bf16[16,32,256]{2,1,0:T(8,128)(2,1)S(1)} %bitcast.42), channel_id=1, replica_groups=mesh['z'=16,'y'=4,'c'=2,'x'=4] {'z'}, dimensions={0} | all-to-all | bytes 524288 | tf_op jit(solution)/shard_map/all_to_all | solution.py:337
  58.0 0.7 spread.1
  58.7 0.0 copy-start.6
  58.7 27.1 %all_to_all.66 = bf16[32,96,256]{2,1,0:T(8,128)(2,1)S(1)} all-to-all(bf16[32,96,256]{2,1,0:T(8,128)(2,1)S(1)} %bitcast.32), channel_id=1, replica_groups=mesh['z'=16,'y'=4,'c'=2,'x'=4] {'y','c','x'}, dimensions={0} | all-to-all | bytes 3145728 | tf_op jit(solution)/shard_map/all_to_all | solution.py:337
  85.8 4.0 %experts.3 = (bf16[8,4,96,256]{3,2,1,0:T(8,128)(2,1)S(1)}, s32[1]{0:T(128)}) custom-call(bf16[8,4,96,256]{3,2,1,0:T(8,128)(2,1)S(1)} %bitcast.33, f32[1,1024]{1,0:T(1,128)S(1)} %bitcast.46, bf16[1024,1024]{1,0:T(8,128)(2,1)S(1)} %bitcast.50, bf16[1024,1024]{1,0:T(8,128)(2,1)S(1)} %bitcast.52), custom_call_target="tpu_custom_call" | custom-call | flops 3221225472 | bytes 8388608 | tf_op jit(solution)/shard_map/experts/pallas_call | solution.py:285
  89.8 26.8 %all_to_all.67 = bf16[32,96,256]{2,1,0:T(8,128)(2,1)S(1)} all-to-all(bf16[32,96,256]{2,1,0:T(8,128)(2,1)S(1)} %bitcast.34), channel_id=1, replica_groups=mesh['z'=16,'y'=4,'c'=2,'x'=4] {'y','c','x'}, dimensions={0} | all-to-all | bytes 3145728 | tf_op jit(solution)/shard_map/all_to_all | solution.py:337
  116.6 1.5 %collect.1 = bf16[512,256]{1,0:T(8,128)(2,1)} custom-call(bf16[8,4,96,256]{3,2,1,0:T(8,128)(2,1)S(1)} %bitcast.29, f32[8,128]{1,0:T(8,128)S(1)} %get-tuple-element.62.source_ref), custom_call_target="tpu_custom_call" | custom-call | flops 1000000 | bytes 1000000 | tf_op jit(solution)/shard_map/collect/pallas_call | solution.py:49
  118.0 5.3 %all-to-all-start.8 = ((bf16[16,32,256]{2,1,0:T(8,128)(2,1)}), bf16[16,32,256]{2,1,0:T(8,128)(2,1)S(1)}, u32[]{:S(2)}, u32[]{:S(2)}) async-start(bf16[16,32,256]{2,1,0:T(8,128)(2,1)} %bitcast.28), calls=%async_computation.8 | async-start | bytes 524288 | tf_op jit(solution)/shard_map/all_to_all | solution.py:337
  124.0 17.5 %all-to-all-done.8 = bf16[16,32,256]{2,1,0:T(8,128)(2,1)S(1)} async-done(((bf16[16,32,256]{2,1,0:T(8,128)(2,1)}), bf16[16,32,256]{2,1,0:T(8,128)(2,1)S(1)}, u32[]{:S(2)}, u32[]{:S(2)}) %all-to-all-start.8) | async-done | bytes 262176 | tf_op jit(solution)/shard_map/all_to_all | solution.py:337
  141.5 0.2 conditional.1
  141.5 0.2 combine.1
  141.8 0.0 copy-start.3
  141.8 0.6 copy-done.3
  (7 shorter events, 0.0 us)
Async XLA Ops:
  0.0 24.7 %copy-start = (bf16[128,1024]{1,0:T(8,128)(2,1)S(1)}, bf16[128,1024]{1,0:T(8,128)(2,1)}, u32[]{:S(2)}) copy-start(bf16[128,1024]{1,0:T(8,128)(2,1)} %input_ref.3) | copy-start | bytes 786436
  0.0 17.0 %copy-start.9 = (s32[128,2]{0,1:T(2,128)S(1)}, s32[128,2]{0,1:T(2,128)}, u32[]{:S(2)}) copy-start(s32[128,2]{0,1:T(2,128)} %param.22) | copy-start | bytes 3076
  0.0 17.0 %copy-start.1 = (f32[128,2]{0,1:T(2,128)S(1)}, f32[128,2]{0,1:T(2,128)}, u32[]{:S(2)}) copy-start(f32[128,2]{0,1:T(2,128)} %param.23) | copy-start | bytes 3076
  0.0 24.7 %copy-start.5 = (f32[1024]{0:T(1024)S(1)}, f32[1024]{0:T(1024)}, u32[]{:S(2)}) copy-start(f32[1024]{0:T(1024)} %param.19) | copy-start | bytes 12292
  0.0 9.5 %collective-permute-start = (bf16[128,256]{1,0:T(8,128)(2,1)}, bf16[128,256]{1,0:T(8,128)(2,1)S(1)}, u32[]{:S(2)}, u32[]{:S(2)}) collective-permute-start(bf16[128,256]{1,0:T(8,128)(2,1)} %glu_ref.3), channel_id=1, source_target_pairs={{4,8},{12,16},{20,24},{28,32},{36,40},{44,48},{52,56},{60,64},{68,... | collective-permute-start | bytes 196616 | tf_op jit(solution)/shard_map/ppermute | solution.py:353
  5.5 4.0 %collective-permute-start.1 = (bf16[16,256]{1,0:T(8,128)(2,1)}, bf16[16,256]{1,0:T(8,128)(2,1)S(1)}, u32[]{:S(2)}, u32[]{:S(2)}) collective-permute-start(bf16[16,256]{1,0:T(8,128)(2,1)} %edge.1), channel_id=1, source_target_pairs={{0,4},{8,12},{16,20},{24,28},{32,36},{40,44},{48,52},{56,60},{64,6... | collective-permute-start | bytes 24584 | tf_op jit(solution)/shard_map/ppermute | solution.py:364
  9.5 0.6 copy-start.4
  9.5 0.6 copy-start.2
  12.7 12.0 %all-to-all-start.4 = ((bf16[4,144,256]{2,1,0:T(8,128)(2,1)}), bf16[4,144,256]{2,1,0:T(8,128)(2,1)S(1)}, u32[]{:S(2)}, u32[]{:S(2)}) async-start(bf16[4,144,256]{2,1,0:T(8,128)(2,1)} %front.1), calls=%async_computation.4 | async-start | bytes 589824 | tf_op jit(solution)/shard_map/all_to_all | solution.py:337
  24.7 61.1 %copy-start.7 = (bf16[1,1024,1024]{2,1,0:T(8,128)(2,1)S(1)}, bf16[1,1024,1024]{2,1,0:T(8,128)(2,1)}, u32[]{:S(2)}) copy-start(bf16[1,1024,1024]{2,1,0:T(8,128)(2,1)} %param.21) | copy-start | bytes 6291460
  58.7 27.1 %copy-start.6 = (bf16[1,1024,1024]{2,1,0:T(8,128)(2,1)S(1)}, bf16[1,1024,1024]{2,1,0:T(8,128)(2,1)}, u32[]{:S(2)}) copy-start(bf16[1,1024,1024]{2,1,0:T(8,128)(2,1)} %param.20) | copy-start | bytes 6291460
  118.0 23.5 %all-to-all-start.8 = ((bf16[16,32,256]{2,1,0:T(8,128)(2,1)}), bf16[16,32,256]{2,1,0:T(8,128)(2,1)S(1)}, u32[]{:S(2)}, u32[]{:S(2)}) async-start(bf16[16,32,256]{2,1,0:T(8,128)(2,1)} %bitcast.28), calls=%async_computation.8 | async-start | bytes 524288 | tf_op jit(solution)/shard_map/all_to_all | solution.py:337
  141.8 0.6 copy-start.3
